TPU v7x, 32 devices: a whole 2x2x4 slice. The times are simulated.
32 devices in a mesh: ex: 4 (over y, x), ey: 2 (over core), lb: 4 (over z).
Axes of the slice: x: 2, y: 2, z: 4, core: 2. Of those that a mesh axis runs over, the one named last changes fastest.
Arguments:
- atmosphere_state: float32 [15, 128, 32, 256], P(None, 'lb', 'ex', 'ey'), may hold values from -6 to 6
- diffusivity: float32 [15], replicated, may hold values from 0.004 to 0.012
- mixing: float32 [127], replicated, may hold values from 0.5 to 50
- relaxation: float32 [128], replicated, may hold values from 0.05 to 0.5
- forcing: float32 [15, 128], replicated, may hold values from -3 to 3
- span_map: int32 [4, 2, 1024], P('ex', 'ey'), may hold values from 0 to 1023, each once within a row
- cost_class: int32 [32, 256], P('ex', 'ey'), may hold values from 0 to 3, as said below
Outputs:
- new_state: float32 [15, 128, 32, 256], P(None, 'lb', 'ex', 'ey')
Inputs may be any that keep to these rules, and one draw needn't show every extreme that they name: `span_map`: each tile's row lists every one of its 1024 columns exactly once. `cost_class`: sunlit columns, a periodic band of 128 consecutive indices along the second direction, the same for every index along the first, have classes 2 or more; all other columns have classes below 2.
All inputs are finite; a program needn't handle non-finite values.
Results may differ from a plain program's by a relative error of at most 0.00011.
Values sent between devices are 32-bit elements; how exact they have to be, the bound alone decides.
A program may use at most 128 MiB of HBM per device.

v0:
```python
import math

import jax
import jax.numpy as jnp
import numpy as np
from jax import lax
from jax.sharding import PartitionSpec as P

STEPS = 2
SUBSTEPS = 4


def padded(cells, sides, width):
    for axis, dim in sides:
        count = lax.axis_size(axis)
        head = lax.slice_in_dim(cells, 0, width, axis=dim)
        tail = lax.slice_in_dim(cells, cells.shape[dim] - width, cells.shape[dim], axis=dim)
        cells = jnp.concatenate(
            [
                lax.ppermute(tail, axis, [(i, (i + 1) % count) for i in range(count)]),
                cells,
                lax.ppermute(head, axis, [((i + 1) % count, i) for i in range(count)]),
            ],
            axis=dim,
        )
    return cells


def second_table():
    inner_root = 1.0 / math.sqrt(5.0)
    gll_nodes = np.array([-1.0, -inner_root, inner_root, 1.0])
    weights = np.array(
        [
            np.prod(
                [gll_nodes[target] - gll_nodes[source] for source in range(4) if source != target]
            )
            for target in range(4)
        ]
    )
    first_table = np.zeros((4, 4))
    for target in range(4):
        for source in range(4):
            if source != target:
                first_table[target, source] = weights[target] / (
                    weights[source] * (gll_nodes[target] - gll_nodes[source])
                )
    for target in range(4):
        first_table[target, target] = -first_table[target].sum()
    return (first_table @ first_table).astype(np.float32)


def derive(field, second, blocked):
    fields, levels, width_x, width_y = field.shape
    along_x = jnp.einsum(
        "ij,flejy->fleiy",
        second,
        field.reshape(fields, levels, width_x // 4, 4, width_y),
        precision=lax.Precision.HIGHEST,
    )
    along_y = jnp.einsum("flxy,yz->flxz", field, blocked, precision=lax.Precision.HIGHEST)
    return along_x.reshape(field.shape) + along_y


def join_edges(extended):
    width_x = extended.shape[2] - 2
    place_x = (jnp.arange(width_x) % 4)[:, None]
    center = extended[:, :, 1:-1, :]
    before = extended[:, :, :-2, :]
    after = extended[:, :, 2:, :]
    values = jnp.where(
        place_x == 3,
        0.5 * (center + after),
        jnp.where(place_x == 0, 0.5 * (center + before), center),
    )
    width_y = values.shape[3] - 2
    place_y = jnp.arange(width_y) % 4
    center = values[..., 1:-1]
    before = values[..., :-2]
    after = values[..., 2:]
    return jnp.where(
        place_y == 3,
        0.5 * (center + after),
        jnp.where(place_y == 0, 0.5 * (center + before), center),
    )


def build_matrix(mixing, relaxation):
    zero = jnp.zeros((1,), jnp.float32)
    diagonal = 1.0 + relaxation + jnp.concatenate([zero, mixing]) + jnp.concatenate([mixing, zero])
    return jnp.diag(diagonal) - jnp.diag(mixing, 1) - jnp.diag(mixing, -1)


def run_physics(columns, marks, factor, forcing):
    levels, fields, count = columns.shape
    classes = marks.astype(jnp.int32)
    push = forcing.T[:, :, None]
    current = columns
    for substep in range(SUBSTEPS):
        active = classes >= substep

        def advance(values, active=active):
            solved = (
                jax.scipy.linalg.cho_solve(
                    (factor, True), values.reshape(levels, fields * count)
                ).reshape(values.shape)
                + push
            )
            return jnp.where(active[None, None, :], solved, values)

        def unchanged(values):
            return values

        current = lax.cond(jnp.any(active), advance, unchanged, current)
    return current


def local(atmosphere_state, diffusivity, mixing, relaxation, forcing, span_map, cost_class):
    fields, slab, width_x, width_y = atmosphere_state.shape
    second_np = second_table()
    second = jnp.asarray(second_np)
    blocked = jnp.asarray(np.kron(np.eye(width_y // 4), second_np.T).astype(np.float32))
    current = atmosphere_state
    for repeat in range(STEPS):
        tendency = derive(current, second, blocked)
        extended = padded(tendency, (("ex", 2), ("ey", 3)), 1)
        current = current + diffusivity[:, None, None, None] * join_edges(extended)
    column_count = width_x * width_y
    flat = current.reshape(fields, slab, column_count)
    order = span_map.reshape(column_count)
    inverse = (
        jnp.zeros((column_count,), jnp.int32)
        .at[order]
        .set(jnp.arange(column_count, dtype=jnp.int32))
    )
    ordered = jnp.take(flat, order, axis=2)
    classes = jnp.take(cost_class.reshape(column_count), order).astype(jnp.float32)
    factor = jnp.linalg.cholesky(build_matrix(mixing, relaxation))
    slabs = lax.axis_size("lb")
    tiles = lax.axis_size("ex") * lax.axis_size("ey")
    levels = slab * slabs
    group = column_count // (tiles * slabs)
    received, marks_in = (
        lax.all_to_all(ordered, ("ex", "ey", "lb"), split_axis=2, concat_axis=2, tiled=True),
        lax.all_to_all(
            classes.reshape(1, 1, column_count),
            ("ex", "ey", "lb"),
            split_axis=2,
            concat_axis=2,
            tiled=True,
        ),
    )
    columns = (
        received.reshape(fields, slab, tiles, slabs, group)
        .transpose(3, 1, 0, 2, 4)
        .reshape(levels, fields, tiles * group)
    )
    marks = marks_in.reshape(tiles, slabs, group)[:, 0, :].reshape(tiles * group)
    physics = run_physics(columns, marks, factor, forcing)
    change = jnp.mean(physics - columns, axis=0).reshape(fields, tiles, group)
    shared = jnp.mean(change, axis=1)
    fixed = physics.reshape(slabs, slab, fields, tiles, group) - shared[None, None, :, None, :]
    outgoing = fixed.transpose(2, 1, 3, 0, 4)
    returned = lax.all_to_all(
        outgoing.reshape(fields, slab, column_count),
        ("ex", "ey", "lb"),
        split_axis=2,
        concat_axis=2,
        tiled=True,
    )
    placed = jnp.take(returned, inverse, axis=2)
    return placed.reshape(fields, slab, width_x, width_y)


def solution(mesh):
    return jax.shard_map(
        local,
        mesh=mesh,
        in_specs=(
            P(None, "lb", "ex", "ey"),
            P(),
            P(),
            P(),
            P(),
            P("ex", "ey", None),
            P("ex", "ey"),
        ),
        out_specs=P(None, "lb", "ex", "ey"),
        check_vma=False,
    )
```

profile of v0, /device:TPU:1, one launch (start us, length us, event | category | flops | bytes accessed | tf_op | source)
XLA Modules:
  0.0 431.8 jit_solution(9815348993078516697)
XLA Ops:
  102.7 13.1 %gather_fusion.1 = f32[1024,15,32]{2,1,0:T(8,128)} fusion(f32[15,32,1024]{1,0,2:T(8,128)} %bitcast.117, s32[1024]{0:T(1024)S(1)} %fusion.46), kind=kCustom, calls=%fused_computation.clone | custom fusion | bytes 3936256 | tf_op jit(solution)/shard_map/jit(_take)/gather | solution.py:135
  115.8 8.7 %fusion.56 = f32[1024,15,32]{2,1,0:T(8,128)} fusion(f32[1024,15,32]{2,1,0:T(8,128)} %gather_fusion.1, pred[1024]{0:T(1024)(128)(4,1)S(1)} %compare_and_fusion.1), kind=kLoop, calls=%fused_computation.125 | loop fusion | flops 491520 | bytes 3933184
  124.4 7.5 %reshape.211 = f32[32,1,15360]{2,1,0:T(1,128)} reshape(f32[1024,15,32]{2,1,0:T(8,128)} %fusion.56) | data formatting | bytes 3932160
  132.0 8.0 %all-to-all-start.1 = ((f32[32,1,15360]{2,1,0:T(1,128)}), f32[32,1,15360]{2,1,0:T(1,128)S(1)}, u32[]{:S(2)}, u32[]{:S(2)}) async-start(f32[32,1,15360]{2,1,0:T(1,128)} %reshape.211), calls=%async_computation.1 | async-start | bytes 3932160 | tf_op jit(solution)/shard_map/all_to_all | solution.py:143
  140.3 11.7 %cholesky.19 = f32[128,128]{1,0:T(8,128)S(1)} custom-call(f32[128,128]{1,0:T(8,128)S(1)} %add_multiply_fusion), custom_call_target="Cholesky" | custom-call | tf_op jit(solution)/shard_map/jit(cholesky)/cholesky | solution.py:137
  159.0 26.4 %all-to-all-done.1 = f32[32,1,15360]{2,1,0:T(1,128)S(1)} async-done(((f32[32,1,15360]{2,1,0:T(1,128)}), f32[32,1,15360]{2,1,0:T(1,128)S(1)}, u32[]{:S(2)}, u32[]{:S(2)}) %all-to-all-start.1) | async-done | bytes 1966112 | tf_op jit(solution)/shard_map/all_to_all | solution.py:143
  187.2 7.0 %reduce.15 = f32[32,15360]{1,0:T(8,128)S(1)} reduce(f32[32,1,15360]{2,1,0:T(1,128)} %copy-done.6, f32[]{:T(128)} %broadcast.218), dimensions={1}, to_apply=%all_to_all.10.reduce_sub_computation | reduce | bytes 3932164 | tf_op jit(solution)/shard_map/all_to_all | solution.py:143
  200.4 10.3 %copy.150 = f32[15,32,8,4,32]{4,3,2,1,0:T(4,128)} copy(f32[15,32,8,4,32]{1,0,4,3,2:T(8,128)} %bitcast.113) | data formatting | bytes 3932160 | tf_op jit(solution)/shard_map/reshape | solution.py:153
  210.7 7.4 %copy.132 = f32[4,32,15,8,32]{4,3,1,0,2:T(8,128)} copy(f32[4,32,15,8,32]{4,0,3,1,2:T(4,128)} %bitcast.110) | data formatting | bytes 3932160 | tf_op jit(solution)/shard_map/transpose | solution.py:154
  224.8 32.6 %conditional.4 = (f32[128,15,256]{0,2,1:T(8,128)S(1)}) conditional(s32[]{:T(128)} %convert_element_type.31, (f32[128,15,256]{2,0,1:T(8,128)}) %tuple.49, (s32[256]{0:T(256)S(1)}, f32[4,32,15,8,32]{4,0,3,1,2:T(4,128)}, f32[128,128]{1,0:T(8,128)S(1)}, f32[128,15,1]{0,1,2:T(8,128)S(1)}, f32[128,15,256]{2,0,1:T(8,128)}, /*index=5*/s32[]{:T(128)}) %tuple.73), branch_computations={%region_6.8_spmd, %region_7.10_spmd} | conditional | flops 1510965504 | bytes 33694760 | solution.py:113
  224.8 9.8 %custom-call.11 = f32[1,128,128]{1,2,0:T(8,128)S(1)} custom-call(f32[1,128,128]{2,1,0:T(8,128)S(1)} %select_bitcast_fusion), custom_call_target="InvertDiagBlocksLowerTriangular" | custom-call | tf_op jit(solution)/shard_map/cond/branch_1_fun/jit(_cho_solve)/triangular_solve | solution.py:103
  257.4 15.6 %conditional.5 = (f32[128,15,256]{0,2,1:T(8,128)S(1)}) conditional(s32[]{:T(128)} %convert_element_type.30, f32[128,15,256]{0,2,1:T(8,128)S(1)} %get-tuple-element.145, (s32[256]{0:T(256)S(1)}, f32[128,15,256]{0,2,1:T(8,128)S(1)}, f32[128,128]{1,0:T(8,128)S(1)}, f32[128,15,1]{0,1,2:T(8,128)S(1)}, s32[]{:T(128)}) %tuple.74), branch_computations={%region_8.11_spmd, %region_9.12_spmd} | conditional | flops 1510965504 | bytes 14033932 | solution.py:113
  257.4 9.8 %custom-call.12 = f32[1,128,128]{1,2,0:T(8,128)S(1)} custom-call(f32[1,128,128]{2,1,0:T(8,128)S(1)} %select_bitcast_fusion.1), custom_call_target="InvertDiagBlocksLowerTriangular" | custom-call | tf_op jit(solution)/shard_map/cond/branch_1_fun/jit(_cho_solve)/triangular_solve | solution.py:103
  273.0 15.8 %conditional.6 = (f32[128,15,256]{0,2,1:T(8,128)S(1)}) conditional(s32[]{:T(128)} %convert_element_type.29, f32[128,15,256]{0,2,1:T(8,128)S(1)} %get-tuple-element.146, (s32[256]{0:T(256)S(1)}, f32[128,15,256]{0,2,1:T(8,128)S(1)}, f32[128,128]{1,0:T(8,128)S(1)}, f32[128,15,1]{0,1,2:T(8,128)S(1)}, s32[]{:T(128)}) %tuple.75), branch_computations={%region_10.13_spmd, %region_11.14_spmd} | conditional | flops 1510965504 | bytes 14033932 | solution.py:113
  273.2 9.8 %custom-call.13 = f32[1,128,128]{1,2,0:T(8,128)S(1)} custom-call(f32[1,128,128]{2,1,0:T(8,128)S(1)} %select_bitcast_fusion.2), custom_call_target="InvertDiagBlocksLowerTriangular" | custom-call | tf_op jit(solution)/shard_map/cond/branch_1_fun/jit(_cho_solve)/triangular_solve | solution.py:103
  288.7 25.5 %conditional.7 = (f32[128,15,256]{2,0,1:T(8,128)}, f32[4,32,15,8,32]{4,3,1,0,2:T(8,128)}) conditional(s32[]{:T(128)} %convert_element_type.28, f32[128,15,256]{0,2,1:T(8,128)S(1)} %get-tuple-element.147, (s32[256]{0:T(256)S(1)}, f32[128,15,256]{0,2,1:T(8,128)S(1)}, f32[128,128]{1,0:T(8,128)S(1)}, f32[128,15,1]{0,1,2:T(8,128)S(1)}) %tuple.76), branch_computations={%region_12.15_spmd, %region_13.16_spmd} | conditional | flops 1510965504 | bytes 21898256 | solution.py:113
  289.0 9.8 %custom-call.14 = f32[1,128,128]{1,2,0:T(8,128)S(1)} custom-call(f32[1,128,128]{2,1,0:T(8,128)S(1)} %select_bitcast_fusion.3), custom_call_target="InvertDiagBlocksLowerTriangular" | custom-call | tf_op jit(solution)/shard_map/cond/branch_1_fun/jit(_cho_solve)/triangular_solve | solution.py:103
  316.8 7.5 %subtract_bitcast_fusion = f32[15,32,8,4,32]{4,2,1,3,0:T(8,128)} fusion(f32[4,32,15,8,32]{4,3,1,0,2:T(8,128)} %get-tuple-element.119, f32[15,32]{1,0:T(8,128)S(1)} %broadcast_multiply_fusion.1), kind=kLoop, calls=%fused_computation.37 | loop fusion | flops 491520 | bytes 3934080 | tf_op jit(solution)/shard_map/transpose | solution.py:162
  324.4 10.2 %copy.151 = f32[15,32,8,4,32]{1,0,4,3,2:T(8,128)} copy(f32[15,32,8,4,32]{4,2,1,3,0:T(8,128)} %subtract_bitcast_fusion) | data formatting | bytes 3932160 | tf_op jit(solution)/shard_map/reshape | solution.py:164
  334.5 7.5 %reshape.213 = f32[32,1,15360]{2,1,0:T(1,128)} reshape(f32[1024,15,32]{2,1,0:T(8,128)} %bitcast.114) | data formatting | bytes 3932160
  350.0 41.0 %all-to-all-done.2 = f32[32,1,15360]{2,1,0:T(1,128)} async-done(((f32[32,1,15360]{2,1,0:T(1,128)}), f32[32,1,15360]{2,1,0:T(1,128)}, u32[]{:S(2)}, u32[]{:S(2)}) %all-to-all-start.2) | async-done | bytes 1966112 | tf_op jit(solution)/shard_map/all_to_all | solution.py:163
  391.1 7.0 %reduce.16 = f32[32,15360]{1,0:T(8,128)S(1)} reduce(f32[32,1,15360]{2,1,0:T(1,128)} %all-to-all-done.2, f32[]{:T(128)} %broadcast.218), dimensions={1}, to_apply=%all_to_all.11.reduce_sub_computation | reduce | bytes 3932164 | tf_op jit(solution)/shard_map/all_to_all | solution.py:163
  404.1 13.1 %gather_fusion.2 = f32[1024,15,32]{2,1,0:T(8,128)} fusion(f32[15,32,1024]{1,0,2:T(8,128)} %bitcast.118, s32[1024]{0:T(1024)S(1)} %fusion.47), kind=kCustom, calls=%fused_computation.1.clone | custom fusion | bytes 3936256 | tf_op jit(solution)/shard_map/jit(_take)/gather | solution.py:170
  417.1 8.7 %broadcast_select_fusion = f32[1024,15,32]{2,1,0:T(8,128)} fusion(f32[1024,15,32]{2,1,0:T(8,128)} %gather_fusion.2, pred[1024]{0:T(1024)(128)(4,1)S(1)} %compare_and_fusion), kind=kLoop, calls=%fused_computation.40 | loop fusion | flops 491520 | bytes 3933184 | tf_op jit(solution)/shard_map/jit(_take)/select_n | solution.py:170
  (132 shorter events, 193.1 us)
Async XLA Ops:
  0.0 31.5 %copy-start = (s32[8,128]{1,0:T(8,128)S(1)}, s32[8,128]{1,0:T(8,128)}, u32[]{:S(2)}) copy-start(s32[8,128]{1,0:T(8,128)} %param.27) | copy-start | bytes 12292
  0.0 5.3 %copy-start.4 = (f32[15,32,8,128]{3,2,1,0:T(8,128)S(1)}, f32[15,32,8,128]{3,2,1,0:T(8,128)}, u32[]{:S(2)}) copy-start(f32[15,32,8,128]{3,2,1,0:T(8,128)} %param.21) | copy-start | bytes 5898244
  0.0 5.3 %copy-start.7 = (f32[128,128,1,1]{1,0,3,2:T(8,128)S(1)}, f32[128,128,1,1]{1,0,3,2:T(8,128)}, u32[]{:S(2)}) copy-start(f32[128,128,1,1]{1,0,3,2:T(8,128)} %constant.152) | copy-start | bytes 196612
  5.3 5.1 %copy-start.9 = (s32[1,1,1024]{2,1,0:T(1,128)S(1)}, s32[1,1,1024]{2,1,0:T(1,128)}, u32[]{:S(2)}) copy-start(s32[1,1,1024]{2,1,0:T(1,128)} %param.26) | copy-start | bytes 12292
  7.3 8.7 %collective-permute-start = (f32[15,32,1,128]{3,1,2,0:T(8,128)S(1)}, f32[15,32,1,128]{3,1,2,0:T(8,128)S(1)}, u32[]{:S(2)}, u32[]{:S(2)}) collective-permute-start(f32[15,32,1,128]{3,1,2,0:T(8,128)S(1)} %get-tuple-element.130), channel_id=1, source_target_pairs={{0,8},{8,16},{16,24},{24,0},{1,9},{9,17},{17,25},{25,1},{2,10},{10... | collective-permute-start | bytes 737288 | tf_op jit(solution)/shard_map/ppermute | solution.py:20
  9.4 11.8 %collective-permute-start.1 = (f32[15,32,1,128]{3,1,2,0:T(8,128)S(1)}, f32[15,32,1,128]{3,1,2,0:T(8,128)S(1)}, u32[]{:S(2)}, u32[]{:S(2)}) collective-permute-start(f32[15,32,1,128]{3,1,2,0:T(8,128)S(1)} %get-tuple-element.131), channel_id=1, source_target_pairs={{8,0},{16,8},{24,16},{0,24},{9,1},{17,9},{25,17},{1,25},{10,2},{18... | collective-permute-start | bytes 737288 | tf_op jit(solution)/shard_map/ppermute | solution.py:22
  27.2 9.1 %collective-permute-start.2 = (f32[15,32,10,1]{1,3,2,0:T(1,128)S(1)}, f32[15,32,10,1]{1,3,2,0:T(1,128)S(1)}, u32[]{:S(2)}, u32[]{:S(2)}) collective-permute-start(f32[15,32,10,1]{1,3,2,0:T(1,128)S(1)} %copy.116), channel_id=1, source_target_pairs={{0,4},{4,0},{1,5},{5,1},{2,6},{6,2},{3,7},{7,3},{8,12},{12,8},{9,1... | collective-permute-start | bytes 57608 | tf_op jit(solution)/shard_map/ppermute | solution.py:20
  31.4 7.2 %collective-permute-start.3 = (f32[15,32,10,1]{1,3,2,0:T(1,128)S(1)}, f32[15,32,10,1]{1,3,2,0:T(1,128)S(1)}, u32[]{:S(2)}, u32[]{:S(2)}) collective-permute-start(f32[15,32,10,1]{1,3,2,0:T(1,128)S(1)} %copy.117), channel_id=1, source_target_pairs={{4,0},{0,4},{5,1},{1,5},{6,2},{2,6},{7,3},{3,7},{12,8},{8,12},{13,... | collective-permute-start | bytes 57608 | tf_op jit(solution)/shard_map/ppermute | solution.py:22
  45.8 1.5 copy-start.5
  45.9 1.5 copy-start.11
  55.2 1.3 copy-start.3
  56.5 8.3 %collective-permute-start.4 = (f32[15,32,1,128]{3,1,2,0:T(8,128)S(1)}, f32[15,32,1,128]{3,1,2,0:T(8,128)S(1)}, u32[]{:S(2)}, u32[]{:S(2)}) collective-permute-start(f32[15,32,1,128]{3,1,2,0:T(8,128)S(1)} %get-tuple-element.128), channel_id=1, source_target_pairs={{0,8},{8,16},{16,24},{24,0},{1,9},{9,17},{17,25},{25,1},{2,10},{10... | collective-permute-start | bytes 737288 | tf_op jit(solution)/shard_map/ppermute | solution.py:20
  57.7 11.0 %collective-permute-start.5 = (f32[15,32,1,128]{3,1,2,0:T(8,128)S(1)}, f32[15,32,1,128]{3,1,2,0:T(8,128)S(1)}, u32[]{:S(2)}, u32[]{:S(2)}) collective-permute-start(f32[15,32,1,128]{3,1,2,0:T(8,128)S(1)} %get-tuple-element.129), channel_id=1, source_target_pairs={{8,0},{16,8},{24,16},{0,24},{9,1},{17,9},{25,17},{1,25},{10,2},{18... | collective-permute-start | bytes 737288 | tf_op jit(solution)/shard_map/ppermute | solution.py:22
  60.0 72.0 %all-to-all-start = ((f32[1,1,1024]{1,0,2:T(1,128)}), f32[1,1,1024]{1,0,2:T(1,128)S(1)}, u32[]{:S(2)}, u32[]{:S(2)}) async-start(f32[1,1,1024]{1,0,2:T(1,128)} %copy.113), calls=%async_computation | async-start | bytes 1048576 | tf_op jit(solution)/shard_map/all_to_all | solution.py:144
  76.3 6.6 %collective-permute-start.6 = (f32[15,32,10,1]{1,3,2,0:T(1,128)S(1)}, f32[15,32,10,1]{1,3,2,0:T(1,128)S(1)}, u32[]{:S(2)}, u32[]{:S(2)}) collective-permute-start(f32[15,32,10,1]{1,3,2,0:T(1,128)S(1)} %copy.125), channel_id=1, source_target_pairs={{0,4},{4,0},{1,5},{5,1},{2,6},{6,2},{3,7},{7,3},{8,12},{12,8},{9,1... | collective-permute-start | bytes 57608 | tf_op jit(solution)/shard_map/ppermute | solution.py:20
  82.7 2.5 collective-permute-start.7
  132.0 8.1 %copy-start.12 = (f32[127]{0:T(128)S(1)}, f32[127]{0:T(128)}, u32[]{:S(2)}) copy-start(f32[127]{0:T(128)} %param.23) | copy-start | bytes 1528
  132.0 8.1 %copy-start.13 = (f32[128]{0:T(128)S(1)}, f32[128]{0:T(128)}, u32[]{:S(2)}) copy-start(f32[128]{0:T(128)} %param.24) | copy-start | bytes 1540
  132.0 53.4 %all-to-all-start.1 = ((f32[32,1,15360]{2,1,0:T(1,128)}), f32[32,1,15360]{2,1,0:T(1,128)S(1)}, u32[]{:S(2)}, u32[]{:S(2)}) async-start(f32[32,1,15360]{2,1,0:T(1,128)} %reshape.211), calls=%async_computation.1 | async-start | bytes 3932160 | tf_op jit(solution)/shard_map/all_to_all | solution.py:143
  185.4 1.3 copy-start.6
  218.1 6.7 %copy-start.8 = (f32[15,128]{1,0:T(8,128)S(1)}, f32[15,128]{1,0:T(8,128)}, u32[]{:S(2)}) copy-start(f32[15,128]{1,0:T(8,128)} %param.25) | copy-start | bytes 23044
  248.1 4.6 %copy-start.2 = (f32[128,15,256]{2,0,1:T(8,128)S(1)}, f32[128,15,256]{2,0,1:T(8,128)}, u32[]{:S(2)}) copy-start(f32[128,15,256]{2,0,1:T(8,128)} %get-tuple-element.114) | copy-start | bytes 5898244 | tf_op jit(solution)/shard_map/cond
  342.0 49.0 %all-to-all-start.2 = ((f32[32,1,15360]{2,1,0:T(1,128)}), f32[32,1,15360]{2,1,0:T(1,128)}, u32[]{:S(2)}, u32[]{:S(2)}) async-start(f32[32,1,15360]{2,1,0:T(1,128)} %reshape.213), calls=%async_computation.2 | async-start | bytes 3932160 | tf_op jit(solution)/shard_map/all_to_all | solution.py:163
  425.8 5.5 %copy-start.1 = (s32[8,128]{1,0:T(8,128)S(1)}, s32[8,128]{1,0:T(8,128)}, u32[]{:S(2)}) copy-start(s32[8,128]{1,0:T(8,128)} %param.27) | copy-start | bytes 12292
  (1 other events, 1.1 us)
where the time goes:
time: 439 us; the launch traced here: 432 us
  local copies, waits for them, and re-layouts  163 us (37%)
  other arithmetic  120 us (27%)
  waiting for transfers between devices  82.2 us (19%)
  matrix products  35.4 us (8%)
  starting transfers between devices  27.5 us (6%)
    all_to_all x1, waiting for transfers between devices, local(): lax.all_to_all(outgoing.reshape(fields, slab, column_count), ('ex', 'ey',...  41 us
    another operation x8, other arithmetic, advance(): jax.scipy.linalg.cho_solve((factor, True), values.reshape(levels, fields...  39.3 us
    unnamed x30, local copies, waits for them, and re-layouts  30.2 us
    all_to_all x1, waiting for transfers between devices, local(): lax.all_to_all(ordered, ('ex', 'ey', 'lb'), split_axis=2, concat_axis=2,...  26.4 us
    another operation x8, matrix products, advance(): jax.scipy.linalg.cho_solve((factor, True), values.reshape(levels, fields...  21.9 us
    gather x1, local copies, waits for them, and re-layouts, local(): ordered = jnp.take(flat, order, axis=2)  13.1 us
    gather x1, local copies, waits for them, and re-layouts, local(): placed = jnp.take(returned, inverse, axis=2)  13.1 us
    another operation x3, other arithmetic, local(): factor = jnp.linalg.cholesky(build_matrix(mixing, relaxation))  12.5 us
  transfers between devices with their start and end apart: 11, of which 5 were waited for; matrix products, arithmetic and copies ran while one was open for 21% of the time, Pallas kernels for 0%

commit v1 on v0

v1 whole, which is shorter than its diff:
```python
import functools
import math

import jax
import jax.numpy as jnp
import numpy as np
from jax import lax
from jax.experimental import pallas as pl
from jax.experimental.pallas import tpu as pltpu
from jax.sharding import PartitionSpec as P

STEPS = 2
SUBSTEPS = 4
MESH = pl.DeviceIdType.MESH
SKEW = 4


def second_table():
    inner_root = 1.0 / math.sqrt(5.0)
    gll_nodes = np.array([-1.0, -inner_root, inner_root, 1.0])
    weights = np.array(
        [
            np.prod(
                [gll_nodes[target] - gll_nodes[source] for source in range(4) if source != target]
            )
            for target in range(4)
        ]
    )
    first_table = np.zeros((4, 4))
    for target in range(4):
        for source in range(4):
            if source != target:
                first_table[target, source] = weights[target] / (
                    weights[source] * (gll_nodes[target] - gll_nodes[source])
                )
    for target in range(4):
        first_table[target, target] = -first_table[target].sum()
    return (first_table @ first_table).astype(np.float32)


def operator_tables(width_x, width_y):
    second = second_table()
    along = np.kron(np.eye(width_y // 4), second.T).astype(np.float64)
    edge = np.zeros((width_y, width_y))
    for y in range(width_y):
        if y % 4 == 3:
            edge[y, y] = 0.5
            if y + 1 < width_y:
                edge[y + 1, y] = 0.5
        elif y % 4 == 0:
            edge[y, y] = 0.5
            if y > 0:
                edge[y - 1, y] = 0.5
        else:
            edge[y, y] = 1.0
    rim = np.zeros((width_y, width_y))
    rim[0, width_y - 1] = 0.5
    rim[width_y - 1, 0] = 0.5
    both = np.concatenate([edge, rim], axis=1)
    weight = np.concatenate([along @ both, both], axis=0).astype(np.float32)
    high = weight.astype(jnp.bfloat16)
    low = (weight - high.astype(np.float32)).astype(jnp.bfloat16)
    shifts = np.zeros((7, width_x, width_y), np.float32)
    for x in range(width_x):
        for d in range(-3, 4):
            if 0 <= x % 4 + d < 4:
                shifts[d + 3, x, :] = second[x % 4, x % 4 + d]
    return high, low, shifts


def series_mul(u, v):
    return [sum(u[i] * v[k - i] for i in range(k + 1)) for k in range(len(u))]


def series_inverse(u):
    first = 1.0 / u[0]
    out = [first]
    for k in range(1, len(u)):
        out.append(-first * sum(u[i] * out[k - i] for i in range(1, k + 1)))
    return out


def prep_kernel(slab, count, params, u_out, sum_out, v_out, coef_out):
    levels = params.shape[1]
    shape = (8, levels)
    lo = jnp.broadcast_to(params[0:1, :], shape)
    hi = jnp.broadcast_to(params[1:2, :], shape)
    rel = jnp.broadcast_to(params[2:3, :], shape)
    lane = lax.broadcasted_iota(jnp.int32, shape, 1)
    row = lax.broadcasted_iota(jnp.int32, shape, 0)
    diag = 1.0 + rel + lo + hi

    def back(x, s):
        return pltpu.roll(x, s, 1)

    def ahead(x, s):
        return pltpu.roll(x, levels - s, 1)

    def reduce_system(a, b, c, extent):
        stages = []
        s = 1
        while s < extent:
            alpha = -a / back(b, s)
            gamma = -c / ahead(b, s)
            b = b + alpha * back(c, s) + gamma * ahead(a, s)
            a = alpha * back(a, s)
            c = gamma * ahead(c, s)
            stages.append((s, alpha, gamma))
            s *= 2
        return stages, 1.0 / b

    def solve(system, d):
        stages, inverse = system
        for s, alpha, gamma in stages:
            d = d + alpha * back(d, s) + gamma * ahead(d, s)
        return d * inverse

    whole = reduce_system(-lo, diag, -hi, levels)
    cut = reduce_system(
        jnp.where(lane % slab == 0, 0.0, -lo),
        diag,
        jnp.where(lane % slab == slab - 1, 0.0, -hi),
        slab,
    )
    push = [params[8:16, :], jnp.where(row == 7, 0.0, params[16:24, :])]
    held = [params[8:16, :], params[16:24, :]]
    for k in range(SUBSTEPS + 1):
        for h in range(2):
            u_out[k * 16 + h * 8 : k * 16 + h * 8 + 8, :] = held[h]
            sum_out[k * 16 + h * 8 : k * 16 + h * 8 + 8, :] = jnp.broadcast_to(
                jnp.sum(held[h], axis=1, keepdims=True), shape
            )
        if k < SUBSTEPS:
            held = [solve(whole, held[h]) + push[h] for h in range(2)]

    spot = jnp.where(row < 4, row * slab + slab - 1, (row - 4) * slab)
    tips = jnp.where((lane == spot) & (row % 4 < count), 1.0, 0.0)
    other = pltpu.roll(tips, 4, 0)

    def total(x):
        return jnp.broadcast_to(jnp.sum(x, axis=1, keepdims=True), shape)

    mix = total(jnp.where(row < 4, lo, hi) * other)
    near, far = [], []
    v = tips
    for k in range(SUBSTEPS):
        v = solve(cut, v)
        v_out[k * 8 : k * 8 + 8, :] = v
        near.append(total(v * tips))
        far.append(total(v * other))
    facing = [pltpu.roll(x, 4, 0) for x in near]
    square = mix * mix
    far_far = series_mul(far, far)

    def beside(z):
        return [jnp.where(row < 4, pltpu.roll(x, 1, 0), pltpu.roll(x, 7, 0)) for x in z]

    def gain(u, v):
        product = series_mul(u, v)
        return series_inverse(
            [(1.0 if k == 0 else 0.0) - square * x for k, x in enumerate(product)]
        )

    z = near
    for _ in range(count - 1):
        zn = beside(z)
        change = series_mul(series_mul(far_far, zn), gain(zn, facing))
        z = [x + square * y for x, y in zip(near, change)]
    zn = beside(z)
    first = [mix * x for x in series_mul(far, gain(zn, facing))]
    next_ = [mix * x for x in series_mul(first, zn)]
    edge = gain(zn, [pltpu.roll(x, 4, 0) for x in z])
    edge_one = [mix * x for x in edge]
    edge_two = [mix * x for x in series_mul(edge_one, zn)]
    for g, part in enumerate((first, next_, edge_one, edge_two)):
        for k in range(SUBSTEPS):
            at = (g * SUBSTEPS + k) * 8
            coef_out[at : at + 8, :] = part[k]


def prep(params, slab, count):
    levels = params.shape[1]
    shapes = [(5 * 16, levels), (5 * 16, levels), (SUBSTEPS * 8, levels), (16 * 8, levels)]
    return pl.pallas_call(
        functools.partial(prep_kernel, slab, count),
        out_shape=[jax.ShapeDtypeStruct(s, jnp.float32) for s in shapes],
        in_specs=[pl.BlockSpec(memory_space=pltpu.VMEM)],
        out_specs=[pl.BlockSpec(memory_space=pltpu.VMEM)] * 4,
    )(params)


def main_kernel(
    dims,
    state, classes, span, w_high, w_low, shifts, rate, u_s, sum_s, v_s, coef_s,
    moved, ends, share,
    lap, hy_out, hy_in, x_out, x_in, weights, p_loc, q_loc, p_out, p_in, q_out, q_in,
    tend, hot, slots, got_one, part, got_two, full,
    ys, yr, xs, xr, ps, pr, qs, qr, os, o_r, ts, t_r, fs, f_r,
):
    n_ex, n_ey, n_lb, fields, slab = dims
    rows = slab * 8
    tiles = n_ex * n_ey
    ex, ey, lb = lax.axis_index("ex"), lax.axis_index("ey"), lax.axis_index("lb")
    tile = ex * n_ey + ey
    sides = 1 if n_ey == 2 else 2

    def tile_peer(o):
        t = lax.rem(tile + o, tiles)
        return (t // n_ey, lax.rem(t, n_ey), lb)

    def slab_peer(o):
        return (ex, ey, lax.rem(lb + o, n_lb))

    barrier = pltpu.get_barrier_semaphore()

    def greet_tiles(o, c):
        pl.semaphore_signal(barrier, inc=1, device_id=tile_peer(o), device_id_type=MESH)
        return c

    def greet_slabs(o, c):
        pl.semaphore_signal(barrier, inc=1, device_id=slab_peer(o), device_id_type=MESH)
        return c

    lax.fori_loop(1, tiles, greet_tiles, 0)
    lax.fori_loop(1, n_lb, greet_slabs, 0)

    row_x = lax.broadcasted_iota(jnp.int32, (8, 128), 0)
    lane = lax.broadcasted_iota(jnp.int32, (8, 128), 1)
    cls = classes[...]

    def derive(f, source, step):
        s = source[f]
        along = shifts[3][None] * s
        for d in (-3, -2, -1, 1, 2, 3):
            along = along + shifts[d + 3][None] * pltpu.roll(s, (8 - d) % 8, 1)
        both = jnp.concatenate([s.reshape(rows, 128), along.reshape(rows, 128)], axis=1)
        high = both.astype(jnp.bfloat16)
        low = (both - high.astype(jnp.float32)).astype(jnp.bfloat16)
        result = (
            jnp.dot(high, w_high[...], preferred_element_type=jnp.float32)
            + jnp.dot(low, w_high[...], preferred_element_type=jnp.float32)
            + jnp.dot(high, w_low[...], preferred_element_type=jnp.float32)
        )
        lap[f] = result[:, :128]
        hy_out[step, f] = result[:, 128:]

    def y_copy(step, f, side):
        peer = lax.rem(ey + (1 if side == 0 else n_ey - 1), n_ey)
        return pltpu.make_async_remote_copy(
            src_ref=hy_out.at[step, f],
            dst_ref=hy_in.at[step, side, f],
            send_sem=ys.at[step, side, f],
            recv_sem=yr.at[step, side, f],
            device_id=(ex, peer, lb),
            device_id_type=MESH,
        )

    def x_copy(step, f, side):
        peer = lax.rem(ex + (1 if side == 0 else n_ex - 1), n_ex)
        return pltpu.make_async_remote_copy(
            src_ref=x_out.at[step, side, f],
            dst_ref=x_in.at[step, side, f],
            send_sem=xs.at[step, side, f],
            recv_sem=xr.at[step, side, f],
            device_id=(peer, ey, lb),
            device_id_type=MESH,
        )

    def start_y(f, step):
        for side in range(sides):
            y_copy(step, f, side).start()

    def spread(step):
        def body(f, c):
            for side in range(sides):
                y_copy(step, f, side).wait_recv()
            value = lap[f].reshape(slab, 8, 128)
            if sides == 1:
                value = value + hy_in[step, 0, f].reshape(slab, 8, 128)
            else:
                value = value + jnp.where(
                    lane == 0, hy_in[step, 0, f].reshape(slab, 8, 128), 0.0
                )
                value = value + jnp.where(
                    lane == 127, hy_in[step, 1, f].reshape(slab, 8, 128), 0.0
                )
            lap[f] = value.reshape(rows, 128)
            x_out[step, 0, f] = lap[f, pl.ds(7, slab, stride=8), :]
            x_out[step, 1, f] = lap[f, pl.ds(0, slab, stride=8), :]
            x_copy(step, f, 0).start()
            x_copy(step, f, 1).start()
            return c

        lax.fori_loop(0, fields, body, 0)

    def advance(f, source, step):
        x_copy(step, f, 0).wait_recv()
        x_copy(step, f, 1).wait_recv()
        value = lap[f].reshape(slab, 8, 128)
        before = pltpu.roll(value, 1, 1)
        after = pltpu.roll(value, 7, 1)
        first = jnp.broadcast_to(x_in[step, 0, f][:, None, :], (slab, 8, 128))
        last = jnp.broadcast_to(x_in[step, 1, f][:, None, :], (slab, 8, 128))
        partner = jnp.where(
            row_x == 0,
            first,
            jnp.where(row_x == 7, last, jnp.where(row_x == 3, after, before)),
        )
        joins = (row_x == 0) | (row_x == 3) | (row_x == 4) | (row_x == 7)
        edged = jnp.where(joins, 0.5 * (value + partner), value)
        moved[f] = source[f] + rate[f] * edged

    derive(0, state, 0)
    pl.semaphore_wait(barrier, tiles - 1 + n_lb - 1)
    start_y(0, 0)

    def open_rest(f, c):
        derive(f, state, 0)
        start_y(f, 0)
        return c

    lax.fori_loop(1, fields, open_rest, 0)
    spread(0)

    def set_weight(l, c):
        at = lb * slab + l
        w = [u_s[k * 16 + 15, at] - 1.0 for k in range(1, 5)]
        weights[l] = jnp.where(
            cls == 0, w[0], jnp.where(cls == 1, w[1], jnp.where(cls == 2, w[2], w[3]))
        )
        return c

    lax.fori_loop(0, slab, set_weight, 0)
    for x in range(8):
        mine = lax.broadcasted_iota(jnp.int32, (128, 1024), 0) + x * 128
        hot[x * 128 : (x + 1) * 128, :] = (
            (mine == span[...]).astype(jnp.float32).astype(jnp.bfloat16)
        )

    def middle(f, c):
        advance(f, state, 0)
        derive(f, moved, 1)
        start_y(f, 1)
        return c

    lax.fori_loop(0, fields, middle, 0)
    spread(1)

    def pick(group, k, base):
        return coef_s[(group * SUBSTEPS + k) * 8 + base + lb, 0]

    def convolve(group, base, k, value):
        out = pick(group, 0, base) * value[k]
        for i in range(1, k + 1):
            out = out + pick(group, i, base) * value[k - i]
        return out

    def scan_copy(f, down):
        if down:
            return pltpu.make_async_remote_copy(
                src_ref=p_out.at[f], dst_ref=p_in.at[f],
                send_sem=ps.at[f], recv_sem=pr.at[f],
                device_id=(ex, ey, lax.rem(lb + 1, n_lb)), device_id_type=MESH,
            )
        return pltpu.make_async_remote_copy(
            src_ref=q_out.at[f], dst_ref=q_in.at[f],
            send_sem=qs.at[f], recv_sem=qr.at[f],
            device_id=(ex, ey, lax.rem(lb + n_lb - 1, n_lb)), device_id_type=MESH,
        )

    def scan_step(f, down):
        arrives = lb > 0 if down else lb < n_lb - 1
        leaves = lb < n_lb - 1 if down else lb > 0
        inward, outward = (p_in, p_out) if down else (q_in, q_out)
        same, opposite = (p_loc, q_loc) if down else (q_loc, p_loc)
        base = 0 if down else 4

        @pl.when((f >= 0) & (f < fields))
        def _():
            @pl.when(arrives)
            def _():
                scan_copy(f, down).wait_recv()
                own = [same[f, k] for k in range(SUBSTEPS)]
                facing = [opposite[f, k] for k in range(SUBSTEPS)]
                coming = [inward[f, k] for k in range(SUBSTEPS)]
                for k in range(SUBSTEPS):
                    outward[f, k] = (
                        own[k] + convolve(0, base, k, coming) + convolve(1, base, k, facing)
                    )

            @pl.when(jnp.logical_not(arrives))
            def _():
                for k in range(SUBSTEPS):
                    outward[f, k] = same[f, k]

            @pl.when(leaves)
            def _():
                scan_copy(f, down).start()

    def scan_steps(i):
        scan_step(i - lb * SKEW, True)
        scan_step(i - (n_lb - 1 - lb) * SKEW, False)

    def summarise(f):
        zero = jnp.zeros((8, 128), jnp.float32)

        def level(l, c):
            x = moved[f, l]
            at = lb * slab + l
            out = [c[k] + v_s[k * 8 + lb, at] * x for k in range(4)]
            out += [c[4 + k] + v_s[k * 8 + 4 + lb, at] * x for k in range(4)]
            out.append(c[8] + weights[l] * x)
            return tuple(out)

        sums = lax.fori_loop(0, slab, level, (zero,) * 9, unroll=8)
        for k in range(SUBSTEPS):
            p_loc[f, k] = sums[k]
            q_loc[f, k] = sums[4 + k]
        h = [sum_s[k * 16 + f, 0] * (1.0 / n_lb) for k in range(4)]
        extra = jnp.where(
            cls == 0, h[0], jnp.where(cls == 1, h[1], jnp.where(cls == 2, h[2], h[3]))
        )
        tend[pl.ds(pl.multiple_of(f * 8, 8), 8), :] = sums[8] + extra

    tend[fields * 8 : 128, :] = jnp.zeros((128 - fields * 8, 128), jnp.float32)

    def closing(i, c):
        advance(i, moved, 1)
        summarise(i)
        scan_steps(i)
        return c

    lax.fori_loop(0, fields, closing, 0)

    def three(value):
        a = value.astype(jnp.bfloat16)
        rest = value - a.astype(jnp.float32)
        b = rest.astype(jnp.bfloat16)
        return a, b, (rest - b.astype(jnp.float32)).astype(jnp.bfloat16)

    span_slots = 1024 // n_lb
    gathered = jnp.zeros((16, 1024), jnp.float32)
    for x in range(8):
        for piece in three(tend[pl.ds(x, 16, stride=8), :]):
            gathered = gathered + jnp.dot(
                piece, hot[x * 128 : (x + 1) * 128, :], preferred_element_type=jnp.float32
            )
    for g in range(n_lb):
        slots[g] = gathered[:, g * span_slots : (g + 1) * span_slots]

    def one_copy(o):
        return pltpu.make_async_remote_copy(
            src_ref=slots.at[lax.rem(lb + o, n_lb)], dst_ref=got_one.at[o - 1],
            send_sem=os.at[o - 1], recv_sem=o_r.at[o - 1],
            device_id=slab_peer(o), device_id_type=MESH,
        )

    def two_copy(o):
        return pltpu.make_async_remote_copy(
            src_ref=part, dst_ref=got_two.at[o - 1],
            send_sem=ts.at[o - 1], recv_sem=t_r.at[o - 1],
            device_id=tile_peer(o), device_id_type=MESH,
        )

    def three_copy(o):
        return pltpu.make_async_remote_copy(
            src_ref=full.at[lb], dst_ref=full.at[lb],
            send_sem=fs.at[o - 1], recv_sem=f_r.at[o - 1],
            device_id=slab_peer(o), device_id_type=MESH,
        )

    def three_arrival(o):
        other = lax.rem(lb + n_lb - o, n_lb)
        return pltpu.make_async_remote_copy(
            src_ref=full.at[other], dst_ref=full.at[other],
            send_sem=fs.at[o - 1], recv_sem=f_r.at[o - 1],
            device_id=slab_peer(o), device_id_type=MESH,
        )

    for o in range(1, n_lb):
        one_copy(o).start()

    tail = (n_lb - 1) * SKEW
    half = fields + tail // 2

    def trailing(i, c):
        scan_steps(i)
        return c

    lax.fori_loop(fields, half, trailing, 0)
    total = slots[lb]
    for o in range(1, n_lb):
        one_copy(o).wait_recv()
        total = total + got_one[o - 1]
    part[...] = total

    def start_two(o, c):
        two_copy(o).start()
        return c

    lax.fori_loop(1, tiles, start_two, 0)
    lax.fori_loop(half, fields + tail, trailing, 0)

    def add_two(o, c):
        two_copy(o).wait_recv()
        return c + got_two[o - 1]

    total = lax.fori_loop(1, tiles, add_two, part[...])
    full[lb] = total * (1.0 / (tiles * slab * n_lb))
    for o in range(1, n_lb):
        three_copy(o).start()

    @pl.when(lb == 0)
    def _():
        p_in[...] = jnp.zeros_like(p_in)

    @pl.when(lb == n_lb - 1)
    def _():
        q_in[...] = jnp.zeros_like(q_in)

    def finish(f, c):
        above = [p_in[f, k] for k in range(SUBSTEPS)]
        below = [q_in[f, k] for k in range(SUBSTEPS)]
        own_p = [p_out[f, k] for k in range(SUBSTEPS)]
        own_q = [q_out[f, k] for k in range(SUBSTEPS)]
        for k in range(SUBSTEPS):
            ends[f, k] = convolve(2, 0, k, above) + convolve(3, 0, k, own_q)
            ends[f, SUBSTEPS + k] = convolve(2, 4, k, below) + convolve(3, 4, k, own_p)
        return c

    lax.fori_loop(0, fields, finish, 0)
    for o in range(1, n_lb):
        three_arrival(o).wait_recv()
    for x in range(8):
        value = jnp.zeros((16, 128), jnp.float32)
        for g in range(n_lb):
            pick_hot = hot[x * 128 : (x + 1) * 128, g * span_slots : (g + 1) * span_slots]
            for piece in three(full[g]):
                value = value + lax.dot_general(
                    piece, pick_hot, (((1,), (1,)), ((), ())),
                    preferred_element_type=jnp.float32,
                )
        share[pl.ds(x, 16, stride=8), :] = value

    def drain(f, c):
        for step in range(STEPS):
            for side in range(sides):
                y_copy(step, f, side).wait_send()
            for side in range(2):
                x_copy(step, f, side).wait_send()

        @pl.when(lb < n_lb - 1)
        def _():
            scan_copy(f, True).wait_send()

        @pl.when(lb > 0)
        def _():
            scan_copy(f, False).wait_send()

        return c

    lax.fori_loop(0, fields, drain, 0)
    for o in range(1, n_lb):
        one_copy(o).wait_send()
        three_copy(o).wait_send()

    def drain_two(o, c):
        two_copy(o).wait_send()
        return c

    lax.fori_loop(1, tiles, drain_two, 0)


def dynamics(dims, state, classes, span, rate, u_t, sum_t, v_t, coef_t):
    n_ex, n_ey, n_lb, fields, slab = dims
    rows = slab * 8
    tiles = n_ex * n_ey
    sides = 1 if n_ey == 2 else 2
    high, low, shifts = operator_tables(8, 128)
    vmem = pl.BlockSpec(memory_space=pltpu.VMEM)
    smem = pl.BlockSpec(memory_space=pltpu.SMEM)
    f32 = jnp.float32
    dma = pltpu.SemaphoreType.DMA
    wide = 1024 // n_lb
    return pl.pallas_call(
        functools.partial(main_kernel, dims),
        out_shape=[
            jax.ShapeDtypeStruct((fields, slab, 8, 128), f32),
            jax.ShapeDtypeStruct((fields, 2 * SUBSTEPS, 8, 128), f32),
            jax.ShapeDtypeStruct((128, 128), f32),
        ],
        in_specs=[vmem] * 6 + [smem] * 5,
        out_specs=[vmem] * 3,
        scratch_shapes=[
            pltpu.VMEM((fields, rows, 128), f32),
            pltpu.VMEM((STEPS, fields, rows, 128), f32),
            pltpu.VMEM((STEPS, sides, fields, rows, 128), f32),
            pltpu.VMEM((STEPS, 2, fields, slab, 128), f32),
            pltpu.VMEM((STEPS, 2, fields, slab, 128), f32),
            pltpu.VMEM((slab, 8, 128), f32),
        ]
        + [pltpu.VMEM((fields, SUBSTEPS, 8, 128), f32)] * 6
        + [
            pltpu.VMEM((128, 128), f32),
            pltpu.VMEM((1024, 1024), jnp.bfloat16),
            pltpu.VMEM((n_lb, 16, wide), f32),
            pltpu.VMEM((n_lb - 1, 16, wide), f32),
            pltpu.VMEM((16, wide), f32),
            pltpu.VMEM((tiles - 1, 16, wide), f32),
            pltpu.VMEM((n_lb, 16, wide), f32),
            dma((STEPS, sides, fields)),
            dma((STEPS, sides, fields)),
            dma((STEPS, 2, fields)),
            dma((STEPS, 2, fields)),
            dma((fields,)),
            dma((fields,)),
            dma((fields,)),
            dma((fields,)),
            dma((n_lb - 1,)),
            dma((n_lb - 1,)),
            dma((tiles - 1,)),
            dma((tiles - 1,)),
            dma((n_lb - 1,)),
            dma((n_lb - 1,)),
        ],
        compiler_params=pltpu.CompilerParams(
            collective_id=0, has_side_effects=True, vmem_limit_bytes=48 * 1024 * 1024
        ),
    )(
        state, classes, span, jnp.asarray(high), jnp.asarray(low), jnp.asarray(shifts),
        rate, u_t, sum_t, v_t, coef_t,
    )


def finish_kernel(
    n_lb, moved, ends, share, classes, params, u_s, out, current, swept, carry, scale, link
):
    group, slab = moved.shape[0], moved.shape[1]
    lb = lax.axis_index("lb")
    step = pl.program_id(0)

    @pl.when(step == 0)
    def _():
        def factor(l, previous):
            at = lb * slab + l
            low = jnp.where(l == 0, 0.0, params[0, at])
            high = jnp.where(l == slab - 1, 0.0, params[1, at])
            ratio = low * previous
            diag = 1.0 + params[2, at] + params[0, at] + params[1, at]
            inverse = 1.0 / (diag - low * ratio)
            carry[l] = ratio
            scale[l] = inverse
            link[l] = high * inverse
            return inverse

        lax.fori_loop(0, slab, factor, jnp.zeros((8, 128), jnp.float32))

    cls = classes[...]
    for k in range(SUBSTEPS):
        source = moved if k == 0 else current

        def down(l, z, source=source):
            z = source[:, l] + carry[l][None] * z
            swept[:, l] = z
            return z

        z = source[:, 0] + ends[:, k]
        swept[:, 0] = z
        z = lax.fori_loop(1, slab, down, z, unroll=4)
        y = (z + ends[:, SUBSTEPS + k]) * scale[slab - 1][None]
        active = cls >= k
        current[:, slab - 1] = jnp.where(active, y, source[:, slab - 1])

        def up(i, y, source=source, active=active):
            l = slab - 1 - i
            y = swept[:, l] * scale[l][None] + link[l][None] * y
            current[:, l] = jnp.where(active, y, source[:, l])
            return y

        lax.fori_loop(1, slab, up, y, unroll=4)

    def close(l, c):
        at = lb * slab + l
        for f in range(group):
            h = [u_s[k * 16 + step * group + f, at] for k in range(4)]
            push = jnp.where(
                cls == 0, h[0], jnp.where(cls == 1, h[1], jnp.where(cls == 2, h[2], h[3]))
            )
            out[f, l] = current[f, l] + (push - share[f])
        return c

    lax.fori_loop(0, slab, close, 0, unroll=2)


def finish(moved, ends, share, classes, params, u_t, n_lb):
    fields, slab = moved.shape[:2]
    group = 5 if fields % 5 == 0 else 1
    f32 = jnp.float32
    return pl.pallas_call(
        functools.partial(finish_kernel, n_lb),
        out_shape=jax.ShapeDtypeStruct(moved.shape, f32),
        grid=(fields // group,),
        in_specs=[
            pl.BlockSpec((group, slab, 8, 128), lambda i: (i, 0, 0, 0)),
            pl.BlockSpec((group, 2 * SUBSTEPS, 8, 128), lambda i: (i, 0, 0, 0)),
            pl.BlockSpec((group, 8, 128), lambda i: (i, 0, 0)),
            pl.BlockSpec((8, 128), lambda i: (0, 0)),
            pl.BlockSpec(memory_space=pltpu.SMEM),
            pl.BlockSpec(memory_space=pltpu.SMEM),
        ],
        out_specs=pl.BlockSpec((group, slab, 8, 128), lambda i: (i, 0, 0, 0)),
        scratch_shapes=[
            pltpu.VMEM((group, slab, 8, 128), f32),
            pltpu.VMEM((group, slab, 8, 128), f32),
            pltpu.VMEM((slab, 8, 128), f32),
            pltpu.VMEM((slab, 8, 128), f32),
            pltpu.VMEM((slab, 8, 128), f32),
        ],
        compiler_params=pltpu.CompilerParams(vmem_limit_bytes=32 * 1024 * 1024),
    )(moved, ends, share, classes, params, u_t)


def local(atmosphere_state, diffusivity, mixing, relaxation, forcing, span_map, cost_class):
    fields, slab, width_x, width_y = atmosphere_state.shape
    n_ex, n_ey, n_lb = (lax.axis_size(a) for a in ("ex", "ey", "lb"))
    levels = slab * n_lb
    zero = jnp.zeros((1,), jnp.float32)
    params = jnp.concatenate(
        [
            jnp.concatenate([zero, mixing])[None],
            jnp.concatenate([mixing, zero])[None],
            relaxation[None],
            jnp.zeros((5, levels), jnp.float32),
            forcing,
            jnp.ones((1, levels), jnp.float32),
        ]
    )
    u_t, sum_t, v_t, coef_t = prep(params, slab, n_lb)
    dims = (n_ex, n_ey, n_lb, fields, slab)
    moved, ends, share = dynamics(
        dims, atmosphere_state, cost_class, span_map.reshape(1, width_x * width_y),
        diffusivity, u_t, sum_t, v_t, coef_t,
    )
    share = share.reshape(16, 8, 128)
    return finish(moved, ends, share, cost_class, params, u_t, n_lb)


def solution(mesh):
    return jax.shard_map(
        local,
        mesh=mesh,
        in_specs=(
            P(None, "lb", "ex", "ey"),
            P(),
            P(),
            P(),
            P(),
            P("ex", "ey", None),
            P("ex", "ey"),
        ),
        out_specs=P(None, "lb", "ex", "ey"),
        check_vma=False,
    )
```

time: 439 us -> 84.9 us (0.19)
  the two profiles are of different devices: /device:TPU:1 before, /device:TPU:0 now
where the time goes in v1:
time: 84.9 us; the launch traced here: 84.2 us
  Pallas kernels  70.3 us (83%)
  local copies, waits for them, and re-layouts  13.1 us (15%)
    pallas_call x1, Pallas kernels, dynamics(): pl.pallas_call(functools.partial(main_kernel, dims), out_shape=[jax.Shape...  56.6 us
    pallas_call x1, Pallas kernels, finish(): pl.pallas_call(functools.partial(finish_kernel, n_lb), out_shape=jax.Shap...  10.1 us
    unnamed x24, local copies, waits for them, and re-layouts  9.24 us
    concatenate x1, local copies, waits for them, and re-layouts, local(): jnp.concatenate([jnp.concatenate([zero, mixing])[None], jnp.concatenate([...  3.83 us
    pallas_call x1, Pallas kernels, prep(): pl.pallas_call(functools.partial(prep_kernel, slab, count), out_shape=[ja...  3.61 us

profile of v1, /device:TPU:0, one launch (start us, length us, event | category | flops | bytes accessed | tf_op | source)
XLA Modules:
  0.0 84.2 jit_solution(15868246381012732351)
XLA Ops:
  0.0 0.8 maximum_bitcast_fusion.1
  0.8 3.8 %concatenate.11.params = f32[24,128]{1,0:T(8,128)} concatenate(f32[1,128]{1,0:T(1,128)S(1)} %get-tuple-element.20, f32[1,128]{1,0:T(1,128)S(1)} %get-tuple-element.19, f32[1,128]{1,0:T(1,128)} %bitcast.9, f32[5,128]{1,0:T(8,128)S(1)} %broadcast_in_dim.18, f32[15,128]{1,0:T(8,128)} %param.14, f32[1,128]{1,0:T(1,128)S(1)} %broadcast_in_dim.19), dimensions={0} | concatenate | bytes 24576 | tf_op jit(solution)/shard_map/concatenate | solution.py:728
  4.6 0.0 copy-start.4
  4.6 3.6 %shard_map.100 = (f32[80,128]{1,0:T(8,128)}, f32[80,128]{1,0:T(8,128)}, f32[32,128]{1,0:T(8,128)}, f32[128,128]{1,0:T(8,128)}) custom-call(f32[24,128]{1,0:T(8,128)} %concatenate.11.params), custom_call_target="tpu_custom_call" | custom-call | tf_op jit(solution)/shard_map/pallas_call | solution.py:184
  8.3 0.0 copy-start
  8.3 1.5 %copy-done = f32[15,32,8,128]{3,2,1,0:T(8,128)S(1)} copy-done((f32[15,32,8,128]{3,2,1,0:T(8,128)S(1)}, f32[15,32,8,128]{3,2,1,0:T(8,128)}, u32[]{:S(2)}) %copy-start) | copy-done | bytes 1966104
  9.8 0.0 copy-start.1
  9.8 0.8 copy-done.1
  10.6 0.0 copy-start.2
  10.6 0.9 %copy-done.2 = bf16[256,256]{1,0:T(8,128)(2,1)S(1)} copy-done((bf16[256,256]{1,0:T(8,128)(2,1)S(1)}, bf16[256,256]{1,0:T(8,128)(2,1)}, u32[]{:S(2)}) %copy-start.2) | copy-done | bytes 131096
  11.5 0.0 copy-start.3
  11.5 0.9 %copy-done.3 = bf16[256,256]{1,0:T(8,128)(2,1)S(1)} copy-done((bf16[256,256]{1,0:T(8,128)(2,1)S(1)}, bf16[256,256]{1,0:T(8,128)(2,1)}, u32[]{:S(2)}) %copy-start.3) | copy-done | bytes 131096
  12.4 0.0 copy-start.5
  12.4 0.8 copy-done.5
  13.2 0.0 copy-start.6
  13.2 0.8 copy-done.6
  14.0 0.7 copy-done.7
  14.8 0.7 copy-done.8
  15.5 0.7 copy-done.9
  16.2 0.7 copy-done.10
  16.9 0.7 copy-done.11
  17.5 56.6 %shard_map.101 = (f32[15,32,8,128]{3,2,1,0:T(8,128)S(1)}, f32[15,8,8,128]{3,2,1,0:T(8,128)S(1)}, f32[128,128]{1,0:T(8,128)S(1)}) custom-call(f32[15,32,8,128]{3,2,1,0:T(8,128)S(1)} %copy-done, s32[8,128]{1,0:T(8,128)S(1)} %copy-done.9, s32[1,1024]{1,0:T(1,128)S(1)} %bitcast.8, bf16[256,256]{1,0:T(8,128)(2,1)S(1)} %copy-done.3, ...), custom_call_target="tpu_custom_call" | custom-call | tf_op jit(solution)/shard_map/pallas_call | solution.py:585
  74.2 0.0 copy-done.4
  74.2 10.1 %shard_map.102 = f32[15,32,8,128]{3,2,1,0:T(8,128)} custom-call(f32[15,32,8,128]{3,2,1,0:T(8,128)S(1)} %get-tuple-element.16.moved, f32[15,8,8,128]{3,2,1,0:T(8,128)S(1)} %get-tuple-element.17.ends, f32[16,8,128]{2,1,0:T(8,128)S(1)} %bitcast.7, s32[8,128]{1,0:T(8,128)S(1)} %copy-done.9, f32[24,128]{1,0:T(8,128)S(1)} %copy-done.4, f32[80,128]{1,0:T(8,128)S(1)} %copy-done.1), custom_call_target="tpu_custom_call" | custom-call | tf_op jit(solution)/shard_map/pallas_call | solution.py:699
  (7 shorter events, 0.0 us)
Async XLA Ops:
  4.6 69.5 %copy-start.4 = (f32[24,128]{1,0:T(8,128)S(1)}, f32[24,128]{1,0:T(8,128)}, u32[]{:S(2)}) copy-start(f32[24,128]{1,0:T(8,128)} %concatenate.11.params) | copy-start | bytes 36868
  8.3 1.5 %copy-start = (f32[15,32,8,128]{3,2,1,0:T(8,128)S(1)}, f32[15,32,8,128]{3,2,1,0:T(8,128)}, u32[]{:S(2)}) copy-start(f32[15,32,8,128]{3,2,1,0:T(8,128)} %state.1) | copy-start | bytes 5898244
  9.8 0.8 copy-start.1
  10.6 0.9 %copy-start.2 = (bf16[256,256]{1,0:T(8,128)(2,1)S(1)}, bf16[256,256]{1,0:T(8,128)(2,1)}, u32[]{:S(2)}) copy-start(bf16[256,256]{1,0:T(8,128)(2,1)} %constant.13.clone.w_low) | copy-start | bytes 393220
  11.5 0.9 %copy-start.3 = (bf16[256,256]{1,0:T(8,128)(2,1)S(1)}, bf16[256,256]{1,0:T(8,128)(2,1)}, u32[]{:S(2)}) copy-start(bf16[256,256]{1,0:T(8,128)(2,1)} %constant.12.clone.w_high) | copy-start | bytes 393220
  12.4 0.8 copy-start.5
  13.2 0.8 copy-start.6
  14.0 0.7 copy-start.7
  14.8 0.7 copy-start.8
  15.5 0.7 copy-start.9
  16.2 0.7 copy-start.10
  16.8 0.7 copy-start.11

commit v2 on v1

--- a/solution.py
+++ b/solution.py
@@ -13,6 +13,7 @@
 SUBSTEPS = 4
 MESH = pl.DeviceIdType.MESH
 SKEW = 4
+VMEM_MIB = 63
 
 
 def second_table():
@@ -58,14 +59,12 @@
     rim[width_y - 1, 0] = 0.5
     both = np.concatenate([edge, rim], axis=1)
     weight = np.concatenate([along @ both, both], axis=0).astype(np.float32)
-    high = weight.astype(jnp.bfloat16)
-    low = (weight - high.astype(np.float32)).astype(jnp.bfloat16)
     shifts = np.zeros((7, width_x, width_y), np.float32)
     for x in range(width_x):
         for d in range(-3, 4):
             if 0 <= x % 4 + d < 4:
                 shifts[d + 3, x, :] = second[x % 4, x % 4 + d]
-    return high, low, shifts
+    return weight, shifts
 
 
 def series_mul(u, v):
@@ -80,12 +79,19 @@
     return out
 
 
-def prep_kernel(slab, count, params, u_out, sum_out, v_out, coef_out):
-    levels = params.shape[1]
+def prepare(slab, count, params, mix_in, relax_in, push_in, u_out, sum_out, v_out, coef_out):
+    levels = relax_in.shape[1]
+    fields = push_in.shape[0]
     shape = (8, levels)
-    lo = jnp.broadcast_to(params[0:1, :], shape)
-    hi = jnp.broadcast_to(params[1:2, :], shape)
-    rel = jnp.broadcast_to(params[2:3, :], shape)
+    params[...] = jnp.zeros_like(params)
+    params[0:1, 0 : levels - 1] = mix_in[...]
+    params[8 : 8 + fields, :] = push_in[...]
+    params[23:24, :] = jnp.ones((1, levels), jnp.float32)
+    hi = jnp.broadcast_to(params[0:1, :], shape)
+    lo = pltpu.roll(hi, 1, 1)
+    rel = jnp.broadcast_to(relax_in[...], shape)
+    params[1:2, :] = relax_in[...]
+    params[2:3, :] = lo[0:1, :]
     lane = lax.broadcasted_iota(jnp.int32, shape, 1)
     row = lax.broadcasted_iota(jnp.int32, shape, 0)
     diag = 1.0 + rel + lo + hi
@@ -124,15 +130,16 @@
     )
     push = [params[8:16, :], jnp.where(row == 7, 0.0, params[16:24, :])]
     held = [params[8:16, :], params[16:24, :]]
+    sums = [jnp.zeros(shape, jnp.float32)] * 2
     for k in range(SUBSTEPS + 1):
         for h in range(2):
             u_out[k * 16 + h * 8 : k * 16 + h * 8 + 8, :] = held[h]
-            sum_out[k * 16 + h * 8 : k * 16 + h * 8 + 8, :] = jnp.broadcast_to(
-                jnp.sum(held[h], axis=1, keepdims=True), shape
-            )
+            sums[h] = jnp.where(lane == k, jnp.sum(held[h], axis=1, keepdims=True), sums[h])
         if k < SUBSTEPS:
             held = [solve(whole, held[h]) + push[h] for h in range(2)]
 
+    sum_out[0:8, :] = sums[0]
+    sum_out[8:16, :] = sums[1]
     spot = jnp.where(row < 4, row * slab + slab - 1, (row - 4) * slab)
     tips = jnp.where((lane == spot) & (row % 4 < count), 1.0, 0.0)
     other = pltpu.roll(tips, 4, 0)
@@ -172,29 +179,23 @@
     edge = gain(zn, [pltpu.roll(x, 4, 0) for x in z])
     edge_one = [mix * x for x in edge]
     edge_two = [mix * x for x in series_mul(edge_one, zn)]
+    packed = jnp.zeros(shape, jnp.float32)
     for g, part in enumerate((first, next_, edge_one, edge_two)):
         for k in range(SUBSTEPS):
-            at = (g * SUBSTEPS + k) * 8
-            coef_out[at : at + 8, :] = part[k]
-
-
-def prep(params, slab, count):
-    levels = params.shape[1]
-    shapes = [(5 * 16, levels), (5 * 16, levels), (SUBSTEPS * 8, levels), (16 * 8, levels)]
-    return pl.pallas_call(
-        functools.partial(prep_kernel, slab, count),
-        out_shape=[jax.ShapeDtypeStruct(s, jnp.float32) for s in shapes],
-        in_specs=[pl.BlockSpec(memory_space=pltpu.VMEM)],
-        out_specs=[pl.BlockSpec(memory_space=pltpu.VMEM)] * 4,
-    )(params)
+            packed = jnp.where(lane == g * SUBSTEPS + k, part[k], packed)
+    coef_out[...] = packed
 
 
 def main_kernel(
     dims,
-    state, classes, span, w_high, w_low, shifts, rate, u_s, sum_s, v_s, coef_s,
-    moved, ends, share,
+    state_h, classes_h, span_h, w_h, shifts_h, rate_h, mix_h, relax_h, push_h,
+    out,
+    state, classes, span, table, weight, shifts, rate, mix_v, relax_v, push_v,
+    params, u_v, sum_v, v_v, coef_v, u_s, sum_s, v_s, coef_s, own_s,
+    moved, swept, carry, scale, link, share,
     lap, hy_out, hy_in, x_out, x_in, weights, p_loc, q_loc, p_out, p_in, q_out, q_in,
     tend, hot, slots, got_one, part, got_two, full,
+    state_sem, in_sem, table_sem,
     ys, yr, xs, xr, ps, pr, qs, qr, os, o_r, ts, t_r, fs, f_r,
 ):
     n_ex, n_ey, n_lb, fields, slab = dims
@@ -221,13 +222,33 @@
         pl.semaphore_signal(barrier, inc=1, device_id=slab_peer(o), device_id_type=MESH)
         return c
 
+    loads = [
+        pltpu.make_async_copy(a, b, in_sem.at[i])
+        for i, (a, b) in enumerate(
+            (
+                (shifts_h, shifts), (w_h, table), (classes_h, classes), (span_h, span),
+                (rate_h, rate), (mix_h, mix_v), (relax_h, relax_v), (push_h, push_v),
+            )
+        )
+    ]
+
+    def load_state(f):
+        return pltpu.make_async_copy(state_h.at[f], state.at[f], state_sem.at[f])
+
+    def fetch(f, c):
+        load_state(f).start()
+        return c
+
+    for copy in loads[:2]:
+        copy.start()
+    lax.fori_loop(0, fields, fetch, 0)
+    for copy in loads[2:]:
+        copy.start()
     lax.fori_loop(1, tiles, greet_tiles, 0)
     lax.fori_loop(1, n_lb, greet_slabs, 0)
 
     row_x = lax.broadcasted_iota(jnp.int32, (8, 128), 0)
     lane = lax.broadcasted_iota(jnp.int32, (8, 128), 1)
-    cls = classes[...]
-
     def derive(f, source, step):
         s = source[f]
         along = shifts[3][None] * s
@@ -237,9 +258,9 @@
         high = both.astype(jnp.bfloat16)
         low = (both - high.astype(jnp.float32)).astype(jnp.bfloat16)
         result = (
-            jnp.dot(high, w_high[...], preferred_element_type=jnp.float32)
-            + jnp.dot(low, w_high[...], preferred_element_type=jnp.float32)
-            + jnp.dot(high, w_low[...], preferred_element_type=jnp.float32)
+            jnp.dot(high, weight[0], preferred_element_type=jnp.float32)
+            + jnp.dot(low, weight[0], preferred_element_type=jnp.float32)
+            + jnp.dot(high, weight[1], preferred_element_type=jnp.float32)
         )
         lap[f] = result[:, :128]
         hy_out[step, f] = result[:, 128:]
@@ -270,28 +291,20 @@
         for side in range(sides):
             y_copy(step, f, side).start()
 
-    def spread(step):
-        def body(f, c):
-            for side in range(sides):
-                y_copy(step, f, side).wait_recv()
-            value = lap[f].reshape(slab, 8, 128)
-            if sides == 1:
-                value = value + hy_in[step, 0, f].reshape(slab, 8, 128)
-            else:
-                value = value + jnp.where(
-                    lane == 0, hy_in[step, 0, f].reshape(slab, 8, 128), 0.0
-                )
-                value = value + jnp.where(
-                    lane == 127, hy_in[step, 1, f].reshape(slab, 8, 128), 0.0
-                )
-            lap[f] = value.reshape(rows, 128)
-            x_out[step, 0, f] = lap[f, pl.ds(7, slab, stride=8), :]
-            x_out[step, 1, f] = lap[f, pl.ds(0, slab, stride=8), :]
-            x_copy(step, f, 0).start()
-            x_copy(step, f, 1).start()
-            return c
-
-        lax.fori_loop(0, fields, body, 0)
+    def spread(f, step):
+        for side in range(sides):
+            y_copy(step, f, side).wait_recv()
+        value = lap[f].reshape(slab, 8, 128)
+        if sides == 1:
+            value = value + hy_in[step, 0, f].reshape(slab, 8, 128)
+        else:
+            value = value + jnp.where(lane == 0, hy_in[step, 0, f].reshape(slab, 8, 128), 0.0)
+            value = value + jnp.where(lane == 127, hy_in[step, 1, f].reshape(slab, 8, 128), 0.0)
+        lap[f] = value.reshape(rows, 128)
+        x_out[step, 0, f] = lap[f, pl.ds(7, slab, stride=8), :]
+        x_out[step, 1, f] = lap[f, pl.ds(0, slab, stride=8), :]
+        x_copy(step, f, 0).start()
+        x_copy(step, f, 1).start()
 
     def advance(f, source, step):
         x_copy(step, f, 0).wait_recv()
@@ -310,17 +323,56 @@
         edged = jnp.where(joins, 0.5 * (value + partner), value)
         moved[f] = source[f] + rate[f] * edged
 
+    for copy in loads[:2]:
+        copy.wait()
+    high = table[...].astype(jnp.bfloat16)
+    weight[0] = high
+    weight[1] = (table[...] - high.astype(jnp.float32)).astype(jnp.bfloat16)
+    load_state(0).wait()
     derive(0, state, 0)
     pl.semaphore_wait(barrier, tiles - 1 + n_lb - 1)
     start_y(0, 0)
 
     def open_rest(f, c):
+        load_state(f).wait()
         derive(f, state, 0)
         start_y(f, 0)
+        spread(f - 1, 0)
         return c
 
     lax.fori_loop(1, fields, open_rest, 0)
-    spread(0)
+    spread(fields - 1, 0)
+    for copy in loads[2:]:
+        copy.wait()
+    cls = classes[...]
+    prepare(slab, n_lb, params, mix_v, relax_v, push_v, u_v, sum_v, v_v, coef_v)
+    own_v = ((u_v, u_s), (sum_v, sum_s), (v_v, v_s), (coef_v, coef_s))
+    tables = [pltpu.make_async_copy(a, b, table_sem.at[i]) for i, (a, b) in enumerate(own_v)]
+    tables.append(pltpu.make_async_copy(params, own_s, table_sem.at[4]))
+    for copy in tables:
+        copy.start()
+    for x in range(8):
+        mine = lax.broadcasted_iota(jnp.int32, (128, 1024), 0) + x * 128
+        hot[x * 128 : (x + 1) * 128, :] = (
+            (mine == span[...]).astype(jnp.float32).astype(jnp.bfloat16)
+        )
+    for copy in tables:
+        copy.wait()
+
+    def factor(l, previous):
+        at = lb * slab + l
+        high = own_s[0, at]
+        low = own_s[2, at]
+        inner_low = jnp.where(l == 0, 0.0, low)
+        inner_high = jnp.where(l == slab - 1, 0.0, high)
+        ratio = inner_low * previous
+        inverse = 1.0 / (1.0 + own_s[1, at] + low + high - inner_low * ratio)
+        carry[l] = ratio
+        scale[l] = inverse
+        link[l] = inner_high * inverse
+        return inverse
+
+    lax.fori_loop(0, slab, factor, jnp.zeros((8, 128), jnp.float32))
 
     def set_weight(l, c):
         at = lb * slab + l
@@ -331,23 +383,22 @@
         return c
 
     lax.fori_loop(0, slab, set_weight, 0)
-    for x in range(8):
-        mine = lax.broadcasted_iota(jnp.int32, (128, 1024), 0) + x * 128
-        hot[x * 128 : (x + 1) * 128, :] = (
-            (mine == span[...]).astype(jnp.float32).astype(jnp.bfloat16)
-        )
-
     def middle(f, c):
         advance(f, state, 0)
         derive(f, moved, 1)
         start_y(f, 1)
+
+        @pl.when(f > 0)
+        def _():
+            spread(f - 1, 1)
+
         return c
 
     lax.fori_loop(0, fields, middle, 0)
-    spread(1)
+    spread(fields - 1, 1)
 
     def pick(group, k, base):
-        return coef_s[(group * SUBSTEPS + k) * 8 + base + lb, 0]
+        return coef_s[base + lb, group * SUBSTEPS + k]
 
     def convolve(group, base, k, value):
         out = pick(group, 0, base) * value[k]
@@ -416,7 +467,7 @@
         for k in range(SUBSTEPS):
             p_loc[f, k] = sums[k]
             q_loc[f, k] = sums[4 + k]
-        h = [sum_s[k * 16 + f, 0] * (1.0 / n_lb) for k in range(4)]
+        h = [sum_s[f, k] * (1.0 / n_lb) for k in range(4)]
         extra = jnp.where(
             cls == 0, h[0], jnp.where(cls == 1, h[1], jnp.where(cls == 2, h[2], h[3]))
         )
@@ -518,17 +569,51 @@
     def _():
         q_in[...] = jnp.zeros_like(q_in)
 
-    def finish(f, c):
-        above = [p_in[f, k] for k in range(SUBSTEPS)]
-        below = [q_in[f, k] for k in range(SUBSTEPS)]
-        own_p = [p_out[f, k] for k in range(SUBSTEPS)]
-        own_q = [q_out[f, k] for k in range(SUBSTEPS)]
+    group = 5 if fields % 5 == 0 else 1
+
+    def sweep(g, c):
+        at = pl.ds(g * group, group)
+        above = [p_in[at, k] for k in range(SUBSTEPS)]
+        below = [q_in[at, k] for k in range(SUBSTEPS)]
+        own_p = [p_out[at, k] for k in range(SUBSTEPS)]
+        own_q = [q_out[at, k] for k in range(SUBSTEPS)]
         for k in range(SUBSTEPS):
-            ends[f, k] = convolve(2, 0, k, above) + convolve(3, 0, k, own_q)
-            ends[f, SUBSTEPS + k] = convolve(2, 4, k, below) + convolve(3, 4, k, own_p)
-        return c
-
-    lax.fori_loop(0, fields, finish, 0)
+            p_loc[at, k] = convolve(2, 0, k, above) + convolve(3, 0, k, own_q)
+            q_loc[at, k] = convolve(2, 4, k, below) + convolve(3, 4, k, own_p)
+        for k in range(SUBSTEPS):
+
+            def down(l, z):
+                z = moved[at, l] + carry[l][None] * z
+                swept[at, l] = z
+                return z
+
+            z = moved[at, 0] + p_loc[at, k]
+            swept[at, 0] = z
+            z = lax.fori_loop(1, slab, down, z, unroll=4)
+            y = (z + q_loc[at, k]) * scale[slab - 1][None]
+            active = cls >= k
+            moved[at, slab - 1] = jnp.where(active, y, moved[at, slab - 1])
+
+            def up(i, y, active=active):
+                l = slab - 1 - i
+                y = swept[at, l] * scale[l][None] + link[l][None] * y
+                moved[at, l] = jnp.where(active, y, moved[at, l])
+                return y
+
+            lax.fori_loop(1, slab, up, y, unroll=4)
+
+        def close(l, c):
+            for f in range(group):
+                h = [u_s[k * 16 + g * group + f, lb * slab + l] for k in range(4)]
+                push = jnp.where(
+                    cls == 0, h[0], jnp.where(cls == 1, h[1], jnp.where(cls == 2, h[2], h[3]))
+                )
+                moved[g * group + f, l] = moved[g * group + f, l] + push
+            return c
+
+        return lax.fori_loop(0, slab, close, c, unroll=2)
+
+    lax.fori_loop(0, fields // group, sweep, 0)
     for o in range(1, n_lb):
         three_arrival(o).wait_recv()
     for x in range(8):
@@ -542,7 +627,18 @@
                 )
         share[pl.ds(x, 16, stride=8), :] = value
 
+    def store(f):
+        return pltpu.make_async_copy(moved.at[f], out.at[f], state_sem.at[f])
+
+    def settle(f, c):
+        moved[f] = moved[f] - share[pl.ds(pl.multiple_of(f * 8, 8), 8), :][None]
+        store(f).start()
+        return c
+
+    lax.fori_loop(0, fields, settle, 0)
+
     def drain(f, c):
+        store(f).wait()
         for step in range(STEPS):
             for side in range(sides):
                 y_copy(step, f, side).wait_send()
@@ -571,27 +667,52 @@
     lax.fori_loop(1, tiles, drain_two, 0)
 
 
-def dynamics(dims, state, classes, span, rate, u_t, sum_t, v_t, coef_t):
-    n_ex, n_ey, n_lb, fields, slab = dims
+def local(atmosphere_state, diffusivity, mixing, relaxation, forcing, span_map, cost_class):
+    fields, slab, width_x, width_y = atmosphere_state.shape
+    n_ex, n_ey, n_lb = (lax.axis_size(a) for a in ("ex", "ey", "lb"))
+    levels = slab * n_lb
+    dims = (n_ex, n_ey, n_lb, fields, slab)
     rows = slab * 8
     tiles = n_ex * n_ey
     sides = 1 if n_ey == 2 else 2
-    high, low, shifts = operator_tables(8, 128)
-    vmem = pl.BlockSpec(memory_space=pltpu.VMEM)
-    smem = pl.BlockSpec(memory_space=pltpu.SMEM)
+    weight, shifts = operator_tables(width_x, width_y)
+    hbm = pl.BlockSpec(memory_space=pltpu.HBM)
     f32 = jnp.float32
     dma = pltpu.SemaphoreType.DMA
     wide = 1024 // n_lb
+    volume = (fields, slab, 8, 128)
     return pl.pallas_call(
         functools.partial(main_kernel, dims),
-        out_shape=[
-            jax.ShapeDtypeStruct((fields, slab, 8, 128), f32),
-            jax.ShapeDtypeStruct((fields, 2 * SUBSTEPS, 8, 128), f32),
-            jax.ShapeDtypeStruct((128, 128), f32),
-        ],
-        in_specs=[vmem] * 6 + [smem] * 5,
-        out_specs=[vmem] * 3,
+        out_shape=jax.ShapeDtypeStruct(volume, f32),
+        in_specs=[hbm] * 9,
+        out_specs=hbm,
         scratch_shapes=[
+            pltpu.VMEM(volume, f32),
+            pltpu.VMEM((8, 128), jnp.int32),
+            pltpu.VMEM((1, 1024), jnp.int32),
+            pltpu.VMEM((256, 256), f32),
+            pltpu.VMEM((2, 256, 256), jnp.bfloat16),
+            pltpu.VMEM((7, 8, 128), f32),
+            pltpu.SMEM((fields,), f32),
+            pltpu.VMEM((1, levels - 1), f32),
+            pltpu.VMEM((1, levels), f32),
+            pltpu.VMEM((fields, levels), f32),
+            pltpu.VMEM((24, levels), f32),
+            pltpu.VMEM((80, levels), f32),
+            pltpu.VMEM((16, levels), f32),
+            pltpu.VMEM((SUBSTEPS * 8, levels), f32),
+            pltpu.VMEM((8, levels), f32),
+            pltpu.SMEM((80, levels), f32),
+            pltpu.SMEM((16, levels), f32),
+            pltpu.SMEM((SUBSTEPS * 8, levels), f32),
+            pltpu.SMEM((8, levels), f32),
+            pltpu.SMEM((24, levels), f32),
+            pltpu.VMEM(volume, f32),
+            pltpu.VMEM(volume, f32),
+            pltpu.VMEM((slab, 8, 128), f32),
+            pltpu.VMEM((slab, 8, 128), f32),
+            pltpu.VMEM((slab, 8, 128), f32),
+            pltpu.VMEM((128, 128), f32),
             pltpu.VMEM((fields, rows, 128), f32),
             pltpu.VMEM((STEPS, fields, rows, 128), f32),
             pltpu.VMEM((STEPS, sides, fields, rows, 128), f32),
@@ -608,6 +729,9 @@
             pltpu.VMEM((16, wide), f32),
             pltpu.VMEM((tiles - 1, 16, wide), f32),
             pltpu.VMEM((n_lb, 16, wide), f32),
+            dma((fields,)),
+            dma((8,)),
+            dma((5,)),
             dma((STEPS, sides, fields)),
             dma((STEPS, sides, fields)),
             dma((STEPS, 2, fields)),
@@ -624,125 +748,13 @@
             dma((n_lb - 1,)),
         ],
         compiler_params=pltpu.CompilerParams(
-            collective_id=0, has_side_effects=True, vmem_limit_bytes=48 * 1024 * 1024
+            collective_id=0, has_side_effects=True, vmem_limit_bytes=VMEM_MIB * 1024 * 1024
         ),
     )(
-        state, classes, span, jnp.asarray(high), jnp.asarray(low), jnp.asarray(shifts),
-        rate, u_t, sum_t, v_t, coef_t,
+        atmosphere_state, cost_class, span_map.reshape(1, width_x * width_y),
+        jnp.asarray(weight), jnp.asarray(shifts), diffusivity,
+        mixing.reshape(1, levels - 1), relaxation.reshape(1, levels), forcing,
     )
-
-
-def finish_kernel(
-    n_lb, moved, ends, share, classes, params, u_s, out, current, swept, carry, scale, link
-):
-    group, slab = moved.shape[0], moved.shape[1]
-    lb = lax.axis_index("lb")
-    step = pl.program_id(0)
-
-    @pl.when(step == 0)
-    def _():
-        def factor(l, previous):
-            at = lb * slab + l
-            low = jnp.where(l == 0, 0.0, params[0, at])
-            high = jnp.where(l == slab - 1, 0.0, params[1, at])
-            ratio = low * previous
-            diag = 1.0 + params[2, at] + params[0, at] + params[1, at]
-            inverse = 1.0 / (diag - low * ratio)
-            carry[l] = ratio
-            scale[l] = inverse
-            link[l] = high * inverse
-            return inverse
-
-        lax.fori_loop(0, slab, factor, jnp.zeros((8, 128), jnp.float32))
-
-    cls = classes[...]
-    for k in range(SUBSTEPS):
-        source = moved if k == 0 else current
-
-        def down(l, z, source=source):
-            z = source[:, l] + carry[l][None] * z
-            swept[:, l] = z
-            return z
-
-        z = source[:, 0] + ends[:, k]
-        swept[:, 0] = z
-        z = lax.fori_loop(1, slab, down, z, unroll=4)
-        y = (z + ends[:, SUBSTEPS + k]) * scale[slab - 1][None]
-        active = cls >= k
-        current[:, slab - 1] = jnp.where(active, y, source[:, slab - 1])
-
-        def up(i, y, source=source, active=active):
-            l = slab - 1 - i
-            y = swept[:, l] * scale[l][None] + link[l][None] * y
-            current[:, l] = jnp.where(active, y, source[:, l])
-            return y
-
-        lax.fori_loop(1, slab, up, y, unroll=4)
-
-    def close(l, c):
-        at = lb * slab + l
-        for f in range(group):
-            h = [u_s[k * 16 + step * group + f, at] for k in range(4)]
-            push = jnp.where(
-                cls == 0, h[0], jnp.where(cls == 1, h[1], jnp.where(cls == 2, h[2], h[3]))
-            )
-            out[f, l] = current[f, l] + (push - share[f])
-        return c
-
-    lax.fori_loop(0, slab, close, 0, unroll=2)
-
-
-def finish(moved, ends, share, classes, params, u_t, n_lb):
-    fields, slab = moved.shape[:2]
-    group = 5 if fields % 5 == 0 else 1
-    f32 = jnp.float32
-    return pl.pallas_call(
-        functools.partial(finish_kernel, n_lb),
-        out_shape=jax.ShapeDtypeStruct(moved.shape, f32),
-        grid=(fields // group,),
-        in_specs=[
-            pl.BlockSpec((group, slab, 8, 128), lambda i: (i, 0, 0, 0)),
-            pl.BlockSpec((group, 2 * SUBSTEPS, 8, 128), lambda i: (i, 0, 0, 0)),
-            pl.BlockSpec((group, 8, 128), lambda i: (i, 0, 0)),
-            pl.BlockSpec((8, 128), lambda i: (0, 0)),
-            pl.BlockSpec(memory_space=pltpu.SMEM),
-            pl.BlockSpec(memory_space=pltpu.SMEM),
-        ],
-        out_specs=pl.BlockSpec((group, slab, 8, 128), lambda i: (i, 0, 0, 0)),
-        scratch_shapes=[
-            pltpu.VMEM((group, slab, 8, 128), f32),
-            pltpu.VMEM((group, slab, 8, 128), f32),
-            pltpu.VMEM((slab, 8, 128), f32),
-            pltpu.VMEM((slab, 8, 128), f32),
-            pltpu.VMEM((slab, 8, 128), f32),
-        ],
-        compiler_params=pltpu.CompilerParams(vmem_limit_bytes=32 * 1024 * 1024),
-    )(moved, ends, share, classes, params, u_t)
-
-
-def local(atmosphere_state, diffusivity, mixing, relaxation, forcing, span_map, cost_class):
-    fields, slab, width_x, width_y = atmosphere_state.shape
-    n_ex, n_ey, n_lb = (lax.axis_size(a) for a in ("ex", "ey", "lb"))
-    levels = slab * n_lb
-    zero = jnp.zeros((1,), jnp.float32)
-    params = jnp.concatenate(
-        [
-            jnp.concatenate([zero, mixing])[None],
-            jnp.concatenate([mixing, zero])[None],
-            relaxation[None],
-            jnp.zeros((5, levels), jnp.float32),
-            forcing,
-            jnp.ones((1, levels), jnp.float32),
-        ]
-    )
-    u_t, sum_t, v_t, coef_t = prep(params, slab, n_lb)
-    dims = (n_ex, n_ey, n_lb, fields, slab)
-    moved, ends, share = dynamics(
-        dims, atmosphere_state, cost_class, span_map.reshape(1, width_x * width_y),
-        diffusivity, u_t, sum_t, v_t, coef_t,
-    )
-    share = share.reshape(16, 8, 128)
-    return finish(moved, ends, share, cost_class, params, u_t, n_lb)
 
 
 def solution(mesh):

time: 84.9 us -> 69.9 us (0.82)
  local copies, waits for them, and re-layouts: 13.1 us -> 2.99 us
  Pallas kernels: 70.3 us -> 66.7 us
    unnamed x24 -> x1, local copies, waits for them, and re-layouts: 9.24 us -> 2.99 us
    concatenate x1 -> x0, local copies, waits for them, and re-layouts: 3.83 us -> none  [local(): jnp.concatenate([jnp.concatenate([zero, mixing])[None], jnp.concatenate([...]
    pallas_call x3 -> x1, Pallas kernels: 70.3 us -> 66.7 us  [local(): pl.pallas_call(functools.partial(main_kernel, dims), out_shape=jax.ShapeD...]
where the time goes in v2:
time: 69.9 us; the launch traced here: 69.7 us
  Pallas kernels  66.7 us (95%)
  local copies, waits for them, and re-layouts  2.99 us (4%)
    pallas_call x1, Pallas kernels, local(): pl.pallas_call(functools.partial(main_kernel, dims), out_shape=jax.ShapeD...  66.7 us
    unnamed x1, local copies, waits for them, and re-layouts  2.99 us

profile of v2, /device:TPU:0, one launch (start us, length us, event | category | flops | bytes accessed | tf_op | source)
XLA Modules:
  0.0 69.7 jit_solution(4397196159650416)
XLA Ops:
  0.0 66.7 %shard_map.91 = f32[15,32,8,128]{3,2,1,0:T(8,128)} custom-call(f32[15,32,8,128]{3,2,1,0:T(8,128)} %state_h.1, s32[8,128]{1,0:T(8,128)} %classes_h.1, s32[1,1024]{1,0:T(1,128)} %bitcast.3, f32[256,256]{1,0:T(8,128)} %constant.4.clone.w_h, f32[7,8,128]{2,1,0:T(8,128)} %constant.5.clone.shifts_h, f32[15]{0:T(128)} %rate_h.1, f32[1,127]{1,0:T(1,128)} %bitcast.4, ...), custom_call_target="tpu_custom_call" | custom-call | tf_op jit(solution)/shard_map/pallas_call | solution.py:684
  66.7 3.0 %copy.11 = f32[15,32,8,128]{3,2,1,0:T(8,128)} copy(f32[15,32,8,128]{3,2,1,0:T(8,128)} %shard_map.91) | data formatting | bytes 3932160

commit v3 on v2

--- a/solution.py
+++ b/solution.py
@@ -12,7 +12,7 @@
 STEPS = 2
 SUBSTEPS = 4
 MESH = pl.DeviceIdType.MESH
-SKEW = 4
+SKEW = 2
 VMEM_MIB = 63
 
 
@@ -204,6 +204,8 @@
     ex, ey, lb = lax.axis_index("ex"), lax.axis_index("ey"), lax.axis_index("lb")
     tile = ex * n_ey + ey
     sides = 1 if n_ey == 2 else 2
+    size = 3 if fields % 3 == 0 else 1
+    chunks = fields // size
 
     def tile_peer(o):
         t = lax.rem(tile + o, tiles)
@@ -232,29 +234,32 @@
         )
     ]
 
+    def chunk(f):
+        return pl.ds(f * size, size)
+
     def load_state(f):
-        return pltpu.make_async_copy(state_h.at[f], state.at[f], state_sem.at[f])
+        return pltpu.make_async_copy(state_h.at[chunk(f)], state.at[chunk(f)], state_sem.at[f])
 
     def fetch(f, c):
         load_state(f).start()
         return c
 
-    for copy in loads[:2]:
+    for copy in loads:
         copy.start()
-    lax.fori_loop(0, fields, fetch, 0)
-    for copy in loads[2:]:
-        copy.start()
+    lax.fori_loop(0, chunks, fetch, 0)
     lax.fori_loop(1, tiles, greet_tiles, 0)
     lax.fori_loop(1, n_lb, greet_slabs, 0)
 
     row_x = lax.broadcasted_iota(jnp.int32, (8, 128), 0)
     lane = lax.broadcasted_iota(jnp.int32, (8, 128), 1)
     def derive(f, source, step):
-        s = source[f]
+        s = source[chunk(f)].reshape(size * slab, 8, 128)
         along = shifts[3][None] * s
         for d in (-3, -2, -1, 1, 2, 3):
             along = along + shifts[d + 3][None] * pltpu.roll(s, (8 - d) % 8, 1)
-        both = jnp.concatenate([s.reshape(rows, 128), along.reshape(rows, 128)], axis=1)
+        both = jnp.concatenate(
+            [s.reshape(size * rows, 128), along.reshape(size * rows, 128)], axis=1
+        )
         high = both.astype(jnp.bfloat16)
         low = (both - high.astype(jnp.float32)).astype(jnp.bfloat16)
         result = (
@@ -262,14 +267,14 @@
             + jnp.dot(low, weight[0], preferred_element_type=jnp.float32)
             + jnp.dot(high, weight[1], preferred_element_type=jnp.float32)
         )
-        lap[f] = result[:, :128]
-        hy_out[step, f] = result[:, 128:]
+        lap[chunk(f)] = result[:, :128].reshape(size, rows, 128)
+        hy_out[step, chunk(f)] = result[:, 128:].reshape(size, rows, 128)
 
     def y_copy(step, f, side):
         peer = lax.rem(ey + (1 if side == 0 else n_ey - 1), n_ey)
         return pltpu.make_async_remote_copy(
-            src_ref=hy_out.at[step, f],
-            dst_ref=hy_in.at[step, side, f],
+            src_ref=hy_out.at[step, chunk(f)],
+            dst_ref=hy_in.at[step, side, chunk(f)],
             send_sem=ys.at[step, side, f],
             recv_sem=yr.at[step, side, f],
             device_id=(ex, peer, lb),
@@ -279,8 +284,8 @@
     def x_copy(step, f, side):
         peer = lax.rem(ex + (1 if side == 0 else n_ex - 1), n_ex)
         return pltpu.make_async_remote_copy(
-            src_ref=x_out.at[step, side, f],
-            dst_ref=x_in.at[step, side, f],
+            src_ref=x_out.at[step, side, chunk(f)],
+            dst_ref=x_in.at[step, side, chunk(f)],
             send_sem=xs.at[step, side, f],
             recv_sem=xr.at[step, side, f],
             device_id=(peer, ey, lb),
@@ -294,40 +299,49 @@
     def spread(f, step):
         for side in range(sides):
             y_copy(step, f, side).wait_recv()
-        value = lap[f].reshape(slab, 8, 128)
+        shape = (size * slab, 8, 128)
+        value = lap[chunk(f)].reshape(shape)
         if sides == 1:
-            value = value + hy_in[step, 0, f].reshape(slab, 8, 128)
+            value = value + hy_in[step, 0, chunk(f)].reshape(shape)
         else:
-            value = value + jnp.where(lane == 0, hy_in[step, 0, f].reshape(slab, 8, 128), 0.0)
-            value = value + jnp.where(lane == 127, hy_in[step, 1, f].reshape(slab, 8, 128), 0.0)
-        lap[f] = value.reshape(rows, 128)
-        x_out[step, 0, f] = lap[f, pl.ds(7, slab, stride=8), :]
-        x_out[step, 1, f] = lap[f, pl.ds(0, slab, stride=8), :]
+            value = value + jnp.where(lane == 0, hy_in[step, 0, chunk(f)].reshape(shape), 0.0)
+            value = value + jnp.where(lane == 127, hy_in[step, 1, chunk(f)].reshape(shape), 0.0)
+        lap[chunk(f)] = value.reshape(size, rows, 128)
+        for i in range(size):
+            x_out[step, 0, f * size + i] = lap[f * size + i, pl.ds(7, slab, stride=8), :]
+            x_out[step, 1, f * size + i] = lap[f * size + i, pl.ds(0, slab, stride=8), :]
         x_copy(step, f, 0).start()
         x_copy(step, f, 1).start()
 
     def advance(f, source, step):
         x_copy(step, f, 0).wait_recv()
         x_copy(step, f, 1).wait_recv()
-        value = lap[f].reshape(slab, 8, 128)
-        before = pltpu.roll(value, 1, 1)
-        after = pltpu.roll(value, 7, 1)
-        first = jnp.broadcast_to(x_in[step, 0, f][:, None, :], (slab, 8, 128))
-        last = jnp.broadcast_to(x_in[step, 1, f][:, None, :], (slab, 8, 128))
-        partner = jnp.where(
-            row_x == 0,
-            first,
-            jnp.where(row_x == 7, last, jnp.where(row_x == 3, after, before)),
-        )
         joins = (row_x == 0) | (row_x == 3) | (row_x == 4) | (row_x == 7)
-        edged = jnp.where(joins, 0.5 * (value + partner), value)
-        moved[f] = source[f] + rate[f] * edged
-
-    for copy in loads[:2]:
+        for i in range(size):
+            g = f * size + i
+            value = lap[g].reshape(slab, 8, 128)
+            before = pltpu.roll(value, 1, 1)
+            after = pltpu.roll(value, 7, 1)
+            first = jnp.broadcast_to(x_in[step, 0, g][:, None, :], (slab, 8, 128))
+            last = jnp.broadcast_to(x_in[step, 1, g][:, None, :], (slab, 8, 128))
+            partner = jnp.where(
+                row_x == 0,
+                first,
+                jnp.where(row_x == 7, last, jnp.where(row_x == 3, after, before)),
+            )
+            edged = jnp.where(joins, 0.5 * (value + partner), value)
+            moved[g] = source[g] + rate[g] * edged
+
+    for copy in loads:
         copy.wait()
-    high = table[...].astype(jnp.bfloat16)
-    weight[0] = high
-    weight[1] = (table[...] - high.astype(jnp.float32)).astype(jnp.bfloat16)
+    prepare(slab, n_lb, params, mix_v, relax_v, push_v, u_v, sum_v, v_v, coef_v)
+    own_v = ((u_v, u_s), (sum_v, sum_s), (v_v, v_s), (coef_v, coef_s), (params, own_s))
+    tables = [pltpu.make_async_copy(a, b, table_sem.at[i]) for i, (a, b) in enumerate(own_v)]
+    for copy in tables:
+        copy.start()
+    split = table[...].astype(jnp.bfloat16)
+    weight[0] = split
+    weight[1] = (table[...] - split.astype(jnp.float32)).astype(jnp.bfloat16)
     load_state(0).wait()
     derive(0, state, 0)
     pl.semaphore_wait(barrier, tiles - 1 + n_lb - 1)
@@ -340,17 +354,9 @@
         spread(f - 1, 0)
         return c
 
-    lax.fori_loop(1, fields, open_rest, 0)
-    spread(fields - 1, 0)
-    for copy in loads[2:]:
-        copy.wait()
+    lax.fori_loop(1, chunks, open_rest, 0)
+    spread(chunks - 1, 0)
     cls = classes[...]
-    prepare(slab, n_lb, params, mix_v, relax_v, push_v, u_v, sum_v, v_v, coef_v)
-    own_v = ((u_v, u_s), (sum_v, sum_s), (v_v, v_s), (coef_v, coef_s))
-    tables = [pltpu.make_async_copy(a, b, table_sem.at[i]) for i, (a, b) in enumerate(own_v)]
-    tables.append(pltpu.make_async_copy(params, own_s, table_sem.at[4]))
-    for copy in tables:
-        copy.start()
     for x in range(8):
         mine = lax.broadcasted_iota(jnp.int32, (128, 1024), 0) + x * 128
         hot[x * 128 : (x + 1) * 128, :] = (
@@ -394,8 +400,8 @@
 
         return c
 
-    lax.fori_loop(0, fields, middle, 0)
-    spread(fields - 1, 1)
+    lax.fori_loop(0, chunks, middle, 0)
+    spread(chunks - 1, 1)
 
     def pick(group, k, base):
         return coef_s[base + lb, group * SUBSTEPS + k]
@@ -409,12 +415,12 @@
     def scan_copy(f, down):
         if down:
             return pltpu.make_async_remote_copy(
-                src_ref=p_out.at[f], dst_ref=p_in.at[f],
+                src_ref=p_out.at[chunk(f)], dst_ref=p_in.at[chunk(f)],
                 send_sem=ps.at[f], recv_sem=pr.at[f],
                 device_id=(ex, ey, lax.rem(lb + 1, n_lb)), device_id_type=MESH,
             )
         return pltpu.make_async_remote_copy(
-            src_ref=q_out.at[f], dst_ref=q_in.at[f],
+            src_ref=q_out.at[chunk(f)], dst_ref=q_in.at[chunk(f)],
             send_sem=qs.at[f], recv_sem=qr.at[f],
             device_id=(ex, ey, lax.rem(lb + n_lb - 1, n_lb)), device_id_type=MESH,
         )
@@ -426,23 +432,23 @@
         same, opposite = (p_loc, q_loc) if down else (q_loc, p_loc)
         base = 0 if down else 4
 
-        @pl.when((f >= 0) & (f < fields))
+        @pl.when((f >= 0) & (f < chunks))
         def _():
             @pl.when(arrives)
             def _():
                 scan_copy(f, down).wait_recv()
-                own = [same[f, k] for k in range(SUBSTEPS)]
-                facing = [opposite[f, k] for k in range(SUBSTEPS)]
-                coming = [inward[f, k] for k in range(SUBSTEPS)]
+                own = [same[chunk(f), k] for k in range(SUBSTEPS)]
+                facing = [opposite[chunk(f), k] for k in range(SUBSTEPS)]
+                coming = [inward[chunk(f), k] for k in range(SUBSTEPS)]
                 for k in range(SUBSTEPS):
-                    outward[f, k] = (
+                    outward[chunk(f), k] = (
                         own[k] + convolve(0, base, k, coming) + convolve(1, base, k, facing)
                     )
 
             @pl.when(jnp.logical_not(arrives))
             def _():
                 for k in range(SUBSTEPS):
-                    outward[f, k] = same[f, k]
+                    outward[chunk(f), k] = same[chunk(f), k]
 
             @pl.when(leaves)
             def _():
@@ -453,25 +459,27 @@
         scan_step(i - (n_lb - 1 - lb) * SKEW, False)
 
     def summarise(f):
-        zero = jnp.zeros((8, 128), jnp.float32)
+        zero = jnp.zeros((size, 8, 128), jnp.float32)
 
         def level(l, c):
-            x = moved[f, l]
+            x = moved[chunk(f), l]
             at = lb * slab + l
             out = [c[k] + v_s[k * 8 + lb, at] * x for k in range(4)]
             out += [c[4 + k] + v_s[k * 8 + 4 + lb, at] * x for k in range(4)]
-            out.append(c[8] + weights[l] * x)
+            out.append(c[8] + weights[l][None] * x)
             return tuple(out)
 
-        sums = lax.fori_loop(0, slab, level, (zero,) * 9, unroll=8)
+        sums = lax.fori_loop(0, slab, level, (zero,) * 9, unroll=4)
         for k in range(SUBSTEPS):
-            p_loc[f, k] = sums[k]
-            q_loc[f, k] = sums[4 + k]
-        h = [sum_s[f, k] * (1.0 / n_lb) for k in range(4)]
-        extra = jnp.where(
-            cls == 0, h[0], jnp.where(cls == 1, h[1], jnp.where(cls == 2, h[2], h[3]))
-        )
-        tend[pl.ds(pl.multiple_of(f * 8, 8), 8), :] = sums[8] + extra
+            p_loc[chunk(f), k] = sums[k]
+            q_loc[chunk(f), k] = sums[4 + k]
+        for i in range(size):
+            g = f * size + i
+            h = [sum_s[g, k] * (1.0 / n_lb) for k in range(4)]
+            extra = jnp.where(
+                cls == 0, h[0], jnp.where(cls == 1, h[1], jnp.where(cls == 2, h[2], h[3]))
+            )
+            tend[pl.ds(pl.multiple_of(g * 8, 8), 8), :] = sums[8][i] + extra
 
     tend[fields * 8 : 128, :] = jnp.zeros((128 - fields * 8, 128), jnp.float32)
 
@@ -481,21 +489,28 @@
         scan_steps(i)
         return c
 
-    lax.fori_loop(0, fields, closing, 0)
+    lax.fori_loop(0, chunks, closing, 0)
 
     def three(value):
         a = value.astype(jnp.bfloat16)
         rest = value - a.astype(jnp.float32)
         b = rest.astype(jnp.bfloat16)
-        return a, b, (rest - b.astype(jnp.float32)).astype(jnp.bfloat16)
+        last = (rest - b.astype(jnp.float32)).astype(jnp.bfloat16)
+        return jnp.concatenate([a, b, last], axis=0)
+
+    def together(value):
+        return value[:16] + value[16:32] + value[32:]
 
     span_slots = 1024 // n_lb
-    gathered = jnp.zeros((16, 1024), jnp.float32)
-    for x in range(8):
-        for piece in three(tend[pl.ds(x, 16, stride=8), :]):
-            gathered = gathered + jnp.dot(
-                piece, hot[x * 128 : (x + 1) * 128, :], preferred_element_type=jnp.float32
-            )
+    gathered = jnp.zeros((48, 1024), jnp.float32)
+    for x in range(0, 8, 2):
+        pair = [three(tend[pl.ds(x + i, 16, stride=8), :]) for i in range(2)]
+        gathered = gathered + jnp.dot(
+            jnp.concatenate(pair, axis=1),
+            hot[x * 128 : (x + 2) * 128, :],
+            preferred_element_type=jnp.float32,
+        )
+    gathered = together(gathered)
     for g in range(n_lb):
         slots[g] = gathered[:, g * span_slots : (g + 1) * span_slots]
 
@@ -531,36 +546,6 @@
     for o in range(1, n_lb):
         one_copy(o).start()
 
-    tail = (n_lb - 1) * SKEW
-    half = fields + tail // 2
-
-    def trailing(i, c):
-        scan_steps(i)
-        return c
-
-    lax.fori_loop(fields, half, trailing, 0)
-    total = slots[lb]
-    for o in range(1, n_lb):
-        one_copy(o).wait_recv()
-        total = total + got_one[o - 1]
-    part[...] = total
-
-    def start_two(o, c):
-        two_copy(o).start()
-        return c
-
-    lax.fori_loop(1, tiles, start_two, 0)
-    lax.fori_loop(half, fields + tail, trailing, 0)
-
-    def add_two(o, c):
-        two_copy(o).wait_recv()
-        return c + got_two[o - 1]
-
-    total = lax.fori_loop(1, tiles, add_two, part[...])
-    full[lb] = total * (1.0 / (tiles * slab * n_lb))
-    for o in range(1, n_lb):
-        three_copy(o).start()
-
     @pl.when(lb == 0)
     def _():
         p_in[...] = jnp.zeros_like(p_in)
@@ -569,10 +554,8 @@
     def _():
         q_in[...] = jnp.zeros_like(q_in)
 
-    group = 5 if fields % 5 == 0 else 1
-
-    def sweep(g, c):
-        at = pl.ds(g * group, group)
+    def sweep(start, group):
+        at = slice(start, start + group)
         above = [p_in[at, k] for k in range(SUBSTEPS)]
         below = [q_in[at, k] for k in range(SUBSTEPS)]
         own_p = [p_out[at, k] for k in range(SUBSTEPS)]
@@ -580,6 +563,22 @@
         for k in range(SUBSTEPS):
             p_loc[at, k] = convolve(2, 0, k, above) + convolve(3, 0, k, own_q)
             q_loc[at, k] = convolve(2, 4, k, below) + convolve(3, 4, k, own_p)
+
+        def push(f, l):
+            h = [u_s[k * 16 + f, lb * slab + l] for k in range(4)]
+            return jnp.where(
+                cls == 0, h[0], jnp.where(cls == 1, h[1], jnp.where(cls == 2, h[2], h[3]))
+            )
+
+        def keep(k, l, y):
+            if k > 0:
+                y = jnp.where(cls >= k, y, moved[at, l])
+            if k < SUBSTEPS - 1:
+                moved[at, l] = y
+            else:
+                for f in range(group):
+                    moved[start + f, l] = y[f] + push(start + f, l)
+
         for k in range(SUBSTEPS):
 
             def down(l, z):
@@ -591,41 +590,66 @@
             swept[at, 0] = z
             z = lax.fori_loop(1, slab, down, z, unroll=4)
             y = (z + q_loc[at, k]) * scale[slab - 1][None]
-            active = cls >= k
-            moved[at, slab - 1] = jnp.where(active, y, moved[at, slab - 1])
-
-            def up(i, y, active=active):
+            keep(k, slab - 1, y)
+
+            def up(i, y, k=k):
                 l = slab - 1 - i
                 y = swept[at, l] * scale[l][None] + link[l][None] * y
-                moved[at, l] = jnp.where(active, y, moved[at, l])
+                keep(k, l, y)
                 return y
 
-            lax.fori_loop(1, slab, up, y, unroll=4)
-
-        def close(l, c):
-            for f in range(group):
-                h = [u_s[k * 16 + g * group + f, lb * slab + l] for k in range(4)]
-                push = jnp.where(
-                    cls == 0, h[0], jnp.where(cls == 1, h[1], jnp.where(cls == 2, h[2], h[3]))
-                )
-                moved[g * group + f, l] = moved[g * group + f, l] + push
-            return c
-
-        return lax.fori_loop(0, slab, close, c, unroll=2)
-
-    lax.fori_loop(0, fields // group, sweep, 0)
+            lax.fori_loop(1, slab, up, y, unroll=4 if k < SUBSTEPS - 1 else 2)
+
+    def trailing(i, c):
+        scan_steps(i)
+        return c
+
+    lax.fori_loop(chunks, chunks + 2, trailing, 0)
+    total = slots[lb]
+    for o in range(1, n_lb):
+        one_copy(o).wait_recv()
+        total = total + got_one[o - 1]
+    part[...] = total
+
+    def start_two(o, c):
+        two_copy(o).start()
+        return c
+
+    lax.fori_loop(1, tiles, start_two, 0)
+    last_step = chunks + (n_lb - 1) * SKEW
+    if fields == 15 and n_lb == 4:
+        lax.fori_loop(chunks + 2, chunks + 3, trailing, 0)
+        sweep(0, 6)
+        lax.fori_loop(chunks + 3, chunks + 4, trailing, 0)
+        sweep(6, 3)
+        lax.fori_loop(chunks + 4, last_step, trailing, 0)
+        rest = (9, 6)
+    else:
+        lax.fori_loop(chunks + 2, last_step, trailing, 0)
+        rest = (0, fields)
+    def add_two(o, c):
+        two_copy(o).wait_recv()
+        return c + got_two[o - 1]
+
+    total = lax.fori_loop(1, tiles, add_two, part[...])
+    full[lb] = total * (1.0 / (tiles * slab * n_lb))
+    for o in range(1, n_lb):
+        three_copy(o).start()
+
+    sweep(*rest)
     for o in range(1, n_lb):
         three_arrival(o).wait_recv()
+    spread_share = jnp.zeros((48, 1024), jnp.float32)
+    for g in range(n_lb):
+        spread_share = spread_share + lax.dot_general(
+            three(full[g]),
+            hot[:, g * span_slots : (g + 1) * span_slots],
+            (((1,), (1,)), ((), ())),
+            preferred_element_type=jnp.float32,
+        )
+    spread_share = together(spread_share)
     for x in range(8):
-        value = jnp.zeros((16, 128), jnp.float32)
-        for g in range(n_lb):
-            pick_hot = hot[x * 128 : (x + 1) * 128, g * span_slots : (g + 1) * span_slots]
-            for piece in three(full[g]):
-                value = value + lax.dot_general(
-                    piece, pick_hot, (((1,), (1,)), ((), ())),
-                    preferred_element_type=jnp.float32,
-                )
-        share[pl.ds(x, 16, stride=8), :] = value
+        share[pl.ds(x, 16, stride=8), :] = spread_share[:, x * 128 : (x + 1) * 128]
 
     def store(f):
         return pltpu.make_async_copy(moved.at[f], out.at[f], state_sem.at[f])
@@ -637,8 +661,13 @@
 
     lax.fori_loop(0, fields, settle, 0)
 
+    def drain_store(f, c):
+        store(f).wait()
+        return c
+
+    lax.fori_loop(0, fields, drain_store, 0)
+
     def drain(f, c):
-        store(f).wait()
         for step in range(STEPS):
             for side in range(sides):
                 y_copy(step, f, side).wait_send()
@@ -655,7 +684,7 @@
 
         return c
 
-    lax.fori_loop(0, fields, drain, 0)
+    lax.fori_loop(0, chunks, drain, 0)
     for o in range(1, n_lb):
         one_copy(o).wait_send()
         three_copy(o).wait_send()

time: 69.9 us -> 54.8 us (0.78)
  Pallas kernels: 66.7 us -> 51.6 us
    pallas_call x1, Pallas kernels: 66.7 us -> 51.6 us  [local(): pl.pallas_call(functools.partial(main_kernel, dims), out_shape=jax.ShapeD...]
where the time goes in v3:
time: 54.8 us; the launch traced here: 54.6 us
  Pallas kernels  51.6 us (94%)
  local copies, waits for them, and re-layouts  2.99 us (5%)
    pallas_call x1, Pallas kernels, local(): pl.pallas_call(functools.partial(main_kernel, dims), out_shape=jax.ShapeD...  51.6 us
    unnamed x1, local copies, waits for them, and re-layouts  2.99 us

profile of v3, /device:TPU:0, one launch (start us, length us, event | category | flops | bytes accessed | tf_op | source)
XLA Modules:
  0.0 54.6 jit_solution(17304397336026483174)
XLA Ops:
  0.0 51.6 %shard_map.91 = f32[15,32,8,128]{3,2,1,0:T(8,128)} custom-call(f32[15,32,8,128]{3,2,1,0:T(8,128)} %state_h.1, s32[8,128]{1,0:T(8,128)} %classes_h.1, s32[1,1024]{1,0:T(1,128)} %bitcast.3, f32[256,256]{1,0:T(8,128)} %constant.4.clone.w_h, f32[7,8,128]{2,1,0:T(8,128)} %constant.5.clone.shifts_h, f32[15]{0:T(128)} %rate_h.1, f32[1,127]{1,0:T(1,128)} %bitcast.4, ...), custom_call_target="tpu_custom_call" | custom-call | tf_op jit(solution)/shard_map/pallas_call | solution.py:713
  51.6 3.0 %copy.11 = f32[15,32,8,128]{3,2,1,0:T(8,128)} copy(f32[15,32,8,128]{3,2,1,0:T(8,128)} %shard_map.91) | data formatting | bytes 3932160

commit v4 on v3

--- a/solution.py
+++ b/solution.py
@@ -12,7 +12,7 @@
 STEPS = 2
 SUBSTEPS = 4
 MESH = pl.DeviceIdType.MESH
-SKEW = 2
+SKEW = 1
 VMEM_MIB = 63
 
 
@@ -189,10 +189,10 @@
 def main_kernel(
     dims,
     state_h, classes_h, span_h, w_h, shifts_h, rate_h, mix_h, relax_h, push_h,
-    out,
+    out, share,
     state, classes, span, table, weight, shifts, rate, mix_v, relax_v, push_v,
     params, u_v, sum_v, v_v, coef_v, u_s, sum_s, v_s, coef_s, own_s,
-    moved, swept, carry, scale, link, share,
+    moved, swept, carry, scale, link,
     lap, hy_out, hy_in, x_out, x_in, weights, p_loc, q_loc, p_out, p_in, q_out, q_in,
     tend, hot, slots, got_one, part, got_two, full,
     state_sem, in_sem, table_sem,
@@ -332,13 +332,8 @@
             edged = jnp.where(joins, 0.5 * (value + partner), value)
             moved[g] = source[g] + rate[g] * edged
 
-    for copy in loads:
+    for copy in loads[:2]:
         copy.wait()
-    prepare(slab, n_lb, params, mix_v, relax_v, push_v, u_v, sum_v, v_v, coef_v)
-    own_v = ((u_v, u_s), (sum_v, sum_s), (v_v, v_s), (coef_v, coef_s), (params, own_s))
-    tables = [pltpu.make_async_copy(a, b, table_sem.at[i]) for i, (a, b) in enumerate(own_v)]
-    for copy in tables:
-        copy.start()
     split = table[...].astype(jnp.bfloat16)
     weight[0] = split
     weight[1] = (table[...] - split.astype(jnp.float32)).astype(jnp.bfloat16)
@@ -356,6 +351,13 @@
 
     lax.fori_loop(1, chunks, open_rest, 0)
     spread(chunks - 1, 0)
+    for copy in loads[2:]:
+        copy.wait()
+    prepare(slab, n_lb, params, mix_v, relax_v, push_v, u_v, sum_v, v_v, coef_v)
+    own_v = ((u_v, u_s), (sum_v, sum_s), (v_v, v_s), (coef_v, coef_s), (params, own_s))
+    tables = [pltpu.make_async_copy(a, b, table_sem.at[i]) for i, (a, b) in enumerate(own_v)]
+    for copy in tables:
+        copy.start()
     cls = classes[...]
     for x in range(8):
         mine = lax.broadcasted_iota(jnp.int32, (128, 1024), 0) + x * 128
@@ -483,13 +485,83 @@
 
     tend[fields * 8 : 128, :] = jnp.zeros((128 - fields * 8, 128), jnp.float32)
 
+    @pl.when(lb == 0)
+    def _():
+        p_in[...] = jnp.zeros_like(p_in)
+
+    @pl.when(lb == n_lb - 1)
+    def _():
+        q_in[...] = jnp.zeros_like(q_in)
+
+    def store(f):
+        return pltpu.make_async_copy(
+            moved.at[chunk(f)], out.at[chunk(f)], state_sem.at[f]
+        )
+
+    def sweep(g):
+        group = size
+        start = g * size
+        at = chunk(g)
+        above = [p_in[at, k] for k in range(SUBSTEPS)]
+        below = [q_in[at, k] for k in range(SUBSTEPS)]
+        own_p = [p_out[at, k] for k in range(SUBSTEPS)]
+        own_q = [q_out[at, k] for k in range(SUBSTEPS)]
+        for k in range(SUBSTEPS):
+            p_loc[at, k] = convolve(2, 0, k, above) + convolve(3, 0, k, own_q)
+            q_loc[at, k] = convolve(2, 4, k, below) + convolve(3, 4, k, own_p)
+
+        def push(f, l):
+            h = [u_s[k * 16 + f, lb * slab + l] for k in range(4)]
+            return jnp.where(
+                cls == 0, h[0], jnp.where(cls == 1, h[1], jnp.where(cls == 2, h[2], h[3]))
+            )
+
+        def keep(k, l, y):
+            if k > 0:
+                y = jnp.where(cls >= k, y, moved[at, l])
+            if k < SUBSTEPS - 1:
+                moved[at, l] = y
+            else:
+                for f in range(group):
+                    moved[start + f, l] = y[f] + push(start + f, l)
+
+        for k in range(SUBSTEPS):
+
+            def down(l, z):
+                z = moved[at, l] + carry[l][None] * z
+                swept[at, l] = z
+                return z
+
+            z = moved[at, 0] + p_loc[at, k]
+            swept[at, 0] = z
+            z = lax.fori_loop(1, slab, down, z, unroll=4)
+            y = (z + q_loc[at, k]) * scale[slab - 1][None]
+            keep(k, slab - 1, y)
+
+            def up(i, y, k=k):
+                l = slab - 1 - i
+                y = swept[at, l] * scale[l][None] + link[l][None] * y
+                keep(k, l, y)
+                return y
+
+            lax.fori_loop(1, slab, up, y, unroll=4 if k < SUBSTEPS - 1 else 2)
+        store(g).start()
+
     def closing(i, c):
         advance(i, moved, 1)
         summarise(i)
         scan_steps(i)
         return c
 
-    lax.fori_loop(0, chunks, closing, 0)
+    hops = (n_lb - 1) * SKEW
+
+    def closing_sweep(i, c):
+        closing(i, c)
+        sweep(i - hops)
+        return c
+
+    lax.fori_loop(0, hops, closing, 0)
+    lax.fori_loop(hops, chunks, closing_sweep, 0)
 
     def three(value):
         a = value.astype(jnp.bfloat16)
@@ -546,65 +618,12 @@
     for o in range(1, n_lb):
         one_copy(o).start()
 
-    @pl.when(lb == 0)
-    def _():
-        p_in[...] = jnp.zeros_like(p_in)
-
-    @pl.when(lb == n_lb - 1)
-    def _():
-        q_in[...] = jnp.zeros_like(q_in)
-
-    def sweep(start, group):
-        at = slice(start, start + group)
-        above = [p_in[at, k] for k in range(SUBSTEPS)]
-        below = [q_in[at, k] for k in range(SUBSTEPS)]
-        own_p = [p_out[at, k] for k in range(SUBSTEPS)]
-        own_q = [q_out[at, k] for k in range(SUBSTEPS)]
-        for k in range(SUBSTEPS):
-            p_loc[at, k] = convolve(2, 0, k, above) + convolve(3, 0, k, own_q)
-            q_loc[at, k] = convolve(2, 4, k, below) + convolve(3, 4, k, own_p)
-
-        def push(f, l):
-            h = [u_s[k * 16 + f, lb * slab + l] for k in range(4)]
-            return jnp.where(
-                cls == 0, h[0], jnp.where(cls == 1, h[1], jnp.where(cls == 2, h[2], h[3]))
-            )
-
-        def keep(k, l, y):
-            if k > 0:
-                y = jnp.where(cls >= k, y, moved[at, l])
-            if k < SUBSTEPS - 1:
-                moved[at, l] = y
-            else:
-                for f in range(group):
-                    moved[start + f, l] = y[f] + push(start + f, l)
-
-        for k in range(SUBSTEPS):
-
-            def down(l, z):
-                z = moved[at, l] + carry[l][None] * z
-                swept[at, l] = z
-                return z
-
-            z = moved[at, 0] + p_loc[at, k]
-            swept[at, 0] = z
-            z = lax.fori_loop(1, slab, down, z, unroll=4)
-            y = (z + q_loc[at, k]) * scale[slab - 1][None]
-            keep(k, slab - 1, y)
-
-            def up(i, y, k=k):
-                l = slab - 1 - i
-                y = swept[at, l] * scale[l][None] + link[l][None] * y
-                keep(k, l, y)
-                return y
-
-            lax.fori_loop(1, slab, up, y, unroll=4 if k < SUBSTEPS - 1 else 2)
-
     def trailing(i, c):
         scan_steps(i)
-        return c
-
-    lax.fori_loop(chunks, chunks + 2, trailing, 0)
+        sweep(i - hops)
+        return c
+
+    lax.fori_loop(chunks, chunks + 1, trailing, 0)
     total = slots[lb]
     for o in range(1, n_lb):
         one_copy(o).wait_recv()
@@ -616,17 +635,8 @@
         return c
 
     lax.fori_loop(1, tiles, start_two, 0)
-    last_step = chunks + (n_lb - 1) * SKEW
-    if fields == 15 and n_lb == 4:
-        lax.fori_loop(chunks + 2, chunks + 3, trailing, 0)
-        sweep(0, 6)
-        lax.fori_loop(chunks + 3, chunks + 4, trailing, 0)
-        sweep(6, 3)
-        lax.fori_loop(chunks + 4, last_step, trailing, 0)
-        rest = (9, 6)
-    else:
-        lax.fori_loop(chunks + 2, last_step, trailing, 0)
-        rest = (0, fields)
+    lax.fori_loop(chunks + 1, chunks + 2, trailing, 0)
+
     def add_two(o, c):
         two_copy(o).wait_recv()
         return c + got_two[o - 1]
@@ -636,7 +646,7 @@
     for o in range(1, n_lb):
         three_copy(o).start()
 
-    sweep(*rest)
+    lax.fori_loop(chunks + 2, chunks + hops, trailing, 0)
     for o in range(1, n_lb):
         three_arrival(o).wait_recv()
     spread_share = jnp.zeros((48, 1024), jnp.float32)
@@ -649,23 +659,13 @@
         )
     spread_share = together(spread_share)
     for x in range(8):
-        share[pl.ds(x, 16, stride=8), :] = spread_share[:, x * 128 : (x + 1) * 128]
-
-    def store(f):
-        return pltpu.make_async_copy(moved.at[f], out.at[f], state_sem.at[f])
-
-    def settle(f, c):
-        moved[f] = moved[f] - share[pl.ds(pl.multiple_of(f * 8, 8), 8), :][None]
-        store(f).start()
-        return c
-
-    lax.fori_loop(0, fields, settle, 0)
+        share[pl.ds(x, fields, stride=8), :] = spread_share[:fields, x * 128 : (x + 1) * 128]
 
     def drain_store(f, c):
         store(f).wait()
         return c
 
-    lax.fori_loop(0, fields, drain_store, 0)
+    lax.fori_loop(0, chunks, drain_store, 0)
 
     def drain(f, c):
         for step in range(STEPS):
@@ -710,11 +710,14 @@
     dma = pltpu.SemaphoreType.DMA
     wide = 1024 // n_lb
     volume = (fields, slab, 8, 128)
-    return pl.pallas_call(
+    physics, share = pl.pallas_call(
         functools.partial(main_kernel, dims),
-        out_shape=jax.ShapeDtypeStruct(volume, f32),
+        out_shape=[
+            jax.ShapeDtypeStruct(volume, f32),
+            jax.ShapeDtypeStruct((fields * 8, 128), f32),
+        ],
         in_specs=[hbm] * 9,
-        out_specs=hbm,
+        out_specs=[hbm, pl.BlockSpec(memory_space=pltpu.VMEM)],
         scratch_shapes=[
             pltpu.VMEM(volume, f32),
             pltpu.VMEM((8, 128), jnp.int32),
@@ -741,7 +744,6 @@
             pltpu.VMEM((slab, 8, 128), f32),
             pltpu.VMEM((slab, 8, 128), f32),
             pltpu.VMEM((slab, 8, 128), f32),
-            pltpu.VMEM((128, 128), f32),
             pltpu.VMEM((fields, rows, 128), f32),
             pltpu.VMEM((STEPS, fields, rows, 128), f32),
             pltpu.VMEM((STEPS, sides, fields, rows, 128), f32),
@@ -784,6 +786,7 @@
         jnp.asarray(weight), jnp.asarray(shifts), diffusivity,
         mixing.reshape(1, levels - 1), relaxation.reshape(1, levels), forcing,
     )
+    return physics - share.reshape(fields, 1, 8, 128)
 
 
 def solution(mesh):

time: 54.8 us -> 58.3 us (1.064)
  Pallas kernels: 51.6 us -> 55.1 us
  other arithmetic: 0 us -> 2.99 us
  local copies, waits for them, and re-layouts: 2.99 us -> 0 us
    pallas_call x1, Pallas kernels: 51.6 us -> 55.1 us  [local(): pl.pallas_call(functools.partial(main_kernel, dims), out_shape=[jax.Shape...]
    unnamed x1 -> x0, local copies, waits for them, and re-layouts: 2.99 us -> none
    sub x0 -> x1, other arithmetic: none -> 2.99 us  [local(): return physics - share.reshape(fields, 1, 8, 128)]
where the time goes in v4:
time: 58.3 us; the launch traced here: 58.1 us
  Pallas kernels  55.1 us (95%)
  other arithmetic  2.99 us (5%)
    pallas_call x1, Pallas kernels, local(): pl.pallas_call(functools.partial(main_kernel, dims), out_shape=[jax.Shape...  55.1 us
    sub x1, other arithmetic, local(): return physics - share.reshape(fields, 1, 8, 128)  2.99 us

profile of v4, /device:TPU:0, one launch (start us, length us, event | category | flops | bytes accessed | tf_op | source)
XLA Modules:
  0.0 58.1 jit_solution(7819443710368663390)
XLA Ops:
  0.0 55.1 %shard_map.91 = (f32[15,32,8,128]{3,2,1,0:T(8,128)}, f32[120,128]{1,0:T(8,128)}) custom-call(f32[15,32,8,128]{3,2,1,0:T(8,128)} %state_h.1, s32[8,128]{1,0:T(8,128)} %classes_h.1, s32[1,1024]{1,0:T(1,128)} %bitcast.5, f32[256,256]{1,0:T(8,128)} %constant.4.clone.w_h, f32[7,8,128]{2,1,0:T(8,128)} %constant.5.clone.shifts_h, f32[15]{0:T(128)} %rate_h.1, ...), custom_call_target="tpu_custom_call" | custom-call | tf_op jit(solution)/shard_map/pallas_call | solution.py:713
  55.1 3.0 %broadcast_subtract_fusion = f32[15,32,8,128]{3,2,1,0:T(8,128)} fusion(f32[15,32,8,128]{3,2,1,0:T(8,128)} %get-tuple-element.7, f32[15,8,128]{2,1,0:T(8,128)} %bitcast.4), kind=kLoop, calls=%fused_computation | loop fusion | flops 491520 | bytes 3993600 | tf_op jit(solution)/shard_map/sub | solution.py:789

commit v5 on v4

--- a/solution.py
+++ b/solution.py
@@ -192,7 +192,7 @@
     out, share,
     state, classes, span, table, weight, shifts, rate, mix_v, relax_v, push_v,
     params, u_v, sum_v, v_v, coef_v, u_s, sum_s, v_s, coef_s, own_s,
-    moved, swept, carry, scale, link,
+    moved, swept, carry, scale, link, middle_scale,
     lap, hy_out, hy_in, x_out, x_in, weights, p_loc, q_loc, p_out, p_in, q_out, q_in,
     tend, hot, slots, got_one, part, got_two, full,
     state_sem, in_sem, table_sem,
@@ -367,20 +367,25 @@
     for copy in tables:
         copy.wait()
 
-    def factor(l, previous):
-        at = lb * slab + l
-        high = own_s[0, at]
-        low = own_s[2, at]
-        inner_low = jnp.where(l == 0, 0.0, low)
-        inner_high = jnp.where(l == slab - 1, 0.0, high)
-        ratio = inner_low * previous
-        inverse = 1.0 / (1.0 + own_s[1, at] + low + high - inner_low * ratio)
-        carry[l] = ratio
-        scale[l] = inverse
-        link[l] = inner_high * inverse
-        return inverse
-
-    lax.fori_loop(0, slab, factor, jnp.zeros((8, 128), jnp.float32))
+    half = slab // 2
+
+    def factor(i, previous):
+        found = []
+        for side, before in enumerate(previous):
+            l = i if side == 0 else slab - 1 - i
+            at = lb * slab + l
+            low, high = own_s[2, at], own_s[0, at]
+            outer, inner = (low, high) if side == 0 else (high, low)
+            ratio = jnp.where(i == 0, 0.0, outer) * before
+            inverse = 1.0 / (1.0 + own_s[1, at] + low + high - jnp.where(i == 0, 0.0, outer) * ratio)
+            carry[l] = ratio
+            scale[l] = inverse
+            link[l] = inner * inverse
+            found.append(inverse)
+        return tuple(found)
+
+    lax.fori_loop(0, half, factor, (jnp.zeros((8, 128), jnp.float32),) * 2)
+    middle_scale[...] = 1.0 / (1.0 - link[half - 1] * link[half])
 
     def set_weight(l, c):
         at = lb * slab + l
@@ -527,24 +532,35 @@
 
         for k in range(SUBSTEPS):
 
-            def down(l, z):
-                z = moved[at, l] + carry[l][None] * z
-                swept[at, l] = z
-                return z
-
-            z = moved[at, 0] + p_loc[at, k]
-            swept[at, 0] = z
-            z = lax.fori_loop(1, slab, down, z, unroll=4)
-            y = (z + q_loc[at, k]) * scale[slab - 1][None]
-            keep(k, slab - 1, y)
-
-            def up(i, y, k=k):
-                l = slab - 1 - i
-                y = swept[at, l] * scale[l][None] + link[l][None] * y
-                keep(k, l, y)
-                return y
-
-            lax.fori_loop(1, slab, up, y, unroll=4 if k < SUBSTEPS - 1 else 2)
+            def inward(i, z):
+                top, low = i, slab - 1 - i
+                above = moved[at, top] + carry[top][None] * z[0]
+                below = moved[at, low] + carry[low][None] * z[1]
+                swept[at, top] = above
+                swept[at, low] = below
+                return above, below
+
+            first = moved[at, 0] + p_loc[at, k]
+            last = moved[at, slab - 1] + q_loc[at, k]
+            swept[at, 0] = first
+            swept[at, slab - 1] = last
+            first, last = lax.fori_loop(1, half, inward, (first, last), unroll=5)
+            first = first * scale[half - 1][None]
+            last = last * scale[half][None]
+            above = (first + link[half - 1][None] * last) * middle_scale[...][None]
+            below = last + link[half][None] * above
+            keep(k, half - 1, above)
+            keep(k, half, below)
+
+            def outward(i, y, k=k):
+                top, low = half - 1 - i, half + i
+                above = swept[at, top] * scale[top][None] + link[top][None] * y[0]
+                below = swept[at, low] * scale[low][None] + link[low][None] * y[1]
+                keep(k, top, above)
+                keep(k, low, below)
+                return above, below
+
+            lax.fori_loop(1, half, outward, (above, below), unroll=5 if k < SUBSTEPS - 1 else 3)
         store(g).start()
 
     def closing(i, c):
@@ -744,6 +760,7 @@
             pltpu.VMEM((slab, 8, 128), f32),
             pltpu.VMEM((slab, 8, 128), f32),
             pltpu.VMEM((slab, 8, 128), f32),
+            pltpu.VMEM((8, 128), f32),
             pltpu.VMEM((fields, rows, 128), f32),
             pltpu.VMEM((STEPS, fields, rows, 128), f32),
             pltpu.VMEM((STEPS, sides, fields, rows, 128), f32),

time: 58.3 us -> 57.9 us (level)
  no operation moved by 1% of the time
where the time goes in v5:
time: 57.9 us; the launch traced here: 57.7 us
  Pallas kernels  54.7 us (94%)
  other arithmetic  2.99 us (5%)
    pallas_call x1, Pallas kernels, local(): pl.pallas_call(functools.partial(main_kernel, dims), out_shape=[jax.Shape...  54.7 us
    sub x1, other arithmetic, local(): return physics - share.reshape(fields, 1, 8, 128)  2.99 us

profile of v5, /device:TPU:0, one launch (start us, length us, event | category | flops | bytes accessed | tf_op | source)
XLA Modules:
  0.0 57.7 jit_solution(16432281325131656627)
XLA Ops:
  0.0 54.7 %shard_map.91 = (f32[15,32,8,128]{3,2,1,0:T(8,128)}, f32[120,128]{1,0:T(8,128)}) custom-call(f32[15,32,8,128]{3,2,1,0:T(8,128)} %state_h.1, s32[8,128]{1,0:T(8,128)} %classes_h.1, s32[1,1024]{1,0:T(1,128)} %bitcast.5, f32[256,256]{1,0:T(8,128)} %constant.4.clone.w_h, f32[7,8,128]{2,1,0:T(8,128)} %constant.5.clone.shifts_h, f32[15]{0:T(128)} %rate_h.1, ...), custom_call_target="tpu_custom_call" | custom-call | tf_op jit(solution)/shard_map/pallas_call | solution.py:729
  54.8 3.0 %broadcast_subtract_fusion = f32[15,32,8,128]{3,2,1,0:T(8,128)} fusion(f32[15,32,8,128]{3,2,1,0:T(8,128)} %get-tuple-element.7, f32[15,8,128]{2,1,0:T(8,128)} %bitcast.4), kind=kLoop, calls=%fused_computation | loop fusion | flops 491520 | bytes 3993600 | tf_op jit(solution)/shard_map/sub | solution.py:806

commit v6 on v5

--- a/solution.py
+++ b/solution.py
@@ -12,7 +12,7 @@
 STEPS = 2
 SUBSTEPS = 4
 MESH = pl.DeviceIdType.MESH
-SKEW = 1
+SKEW = 2
 VMEM_MIB = 63
 
 
@@ -571,13 +571,7 @@
 
     hops = (n_lb - 1) * SKEW
 
-    def closing_sweep(i, c):
-        closing(i, c)
-        sweep(i - hops)
-        return c
-
-    lax.fori_loop(0, hops, closing, 0)
-    lax.fori_loop(hops, chunks, closing_sweep, 0)
+    lax.fori_loop(0, chunks, closing, 0)
 
     def three(value):
         a = value.astype(jnp.bfloat16)
@@ -636,10 +630,14 @@
 
     def trailing(i, c):
         scan_steps(i)
-        sweep(i - hops)
-        return c
-
-    lax.fori_loop(chunks, chunks + 1, trailing, 0)
+
+        @pl.when(i >= hops)
+        def _():
+            sweep(i - hops)
+
+        return c
+
+    lax.fori_loop(chunks, chunks + 2, trailing, 0)
     total = slots[lb]
     for o in range(1, n_lb):
         one_copy(o).wait_recv()
@@ -651,7 +649,7 @@
         return c
 
     lax.fori_loop(1, tiles, start_two, 0)
-    lax.fori_loop(chunks + 1, chunks + 2, trailing, 0)
+    lax.fori_loop(chunks + 2, chunks + 4, trailing, 0)
 
     def add_two(o, c):
         two_copy(o).wait_recv()
@@ -662,7 +660,7 @@
     for o in range(1, n_lb):
         three_copy(o).start()
 
-    lax.fori_loop(chunks + 2, chunks + hops, trailing, 0)
+    lax.fori_loop(chunks + 4, chunks + hops, trailing, 0)
     for o in range(1, n_lb):
         three_arrival(o).wait_recv()
     spread_share = jnp.zeros((48, 1024), jnp.float32)

time: 57.9 us -> 51.7 us (0.89)
  Pallas kernels: 54.7 us -> 48.5 us
    pallas_call x1, Pallas kernels: 54.7 us -> 48.5 us  [local(): pl.pallas_call(functools.partial(main_kernel, dims), out_shape=[jax.Shape...]
where the time goes in v6:
time: 51.7 us; the launch traced here: 51.5 us
  Pallas kernels  48.5 us (94%)
  other arithmetic  2.99 us (6%)
    pallas_call x1, Pallas kernels, local(): pl.pallas_call(functools.partial(main_kernel, dims), out_shape=[jax.Shape...  48.5 us
    sub x1, other arithmetic, local(): return physics - share.reshape(fields, 1, 8, 128)  2.99 us

profile of v6, /device:TPU:0, one launch (start us, length us, event | category | flops | bytes accessed | tf_op | source)
XLA Modules:
  0.0 51.5 jit_solution(7472005993415959347)
XLA Ops:
  0.0 48.5 %shard_map.91 = (f32[15,32,8,128]{3,2,1,0:T(8,128)}, f32[120,128]{1,0:T(8,128)}) custom-call(f32[15,32,8,128]{3,2,1,0:T(8,128)} %state_h.1, s32[8,128]{1,0:T(8,128)} %classes_h.1, s32[1,1024]{1,0:T(1,128)} %bitcast.5, f32[256,256]{1,0:T(8,128)} %constant.4.clone.w_h, f32[7,8,128]{2,1,0:T(8,128)} %constant.5.clone.shifts_h, f32[15]{0:T(128)} %rate_h.1, ...), custom_call_target="tpu_custom_call" | custom-call | tf_op jit(solution)/shard_map/pallas_call | solution.py:727
  48.6 3.0 %broadcast_subtract_fusion = f32[15,32,8,128]{3,2,1,0:T(8,128)} fusion(f32[15,32,8,128]{3,2,1,0:T(8,128)} %get-tuple-element.7, f32[15,8,128]{2,1,0:T(8,128)} %bitcast.4), kind=kLoop, calls=%fused_computation | loop fusion | flops 491520 | bytes 3993600 | tf_op jit(solution)/shard_map/sub | solution.py:804

commit v7 on v6

--- a/solution.py
+++ b/solution.py
@@ -12,7 +12,7 @@
 STEPS = 2
 SUBSTEPS = 4
 MESH = pl.DeviceIdType.MESH
-SKEW = 2
+SKEW = 3
 VMEM_MIB = 63
 
 
@@ -801,7 +801,25 @@
         jnp.asarray(weight), jnp.asarray(shifts), diffusivity,
         mixing.reshape(1, levels - 1), relaxation.reshape(1, levels), forcing,
     )
-    return physics - share.reshape(fields, 1, 8, 128)
+    return subtract(physics, share.reshape(fields, 8, 128))
+
+
+def subtract_kernel(physics, share, out):
+    out[...] = physics[...] - share[...][:, None]
+
+
+def subtract(physics, share):
+    fields, slab = physics.shape[:2]
+    size = 3 if fields % 3 == 0 else 1
+    block = pl.BlockSpec((size, slab, 8, 128), lambda i: (i, 0, 0, 0))
+    return pl.pallas_call(
+        subtract_kernel,
+        out_shape=jax.ShapeDtypeStruct(physics.shape, physics.dtype),
+        grid=(fields // size,),
+        in_specs=[block, pl.BlockSpec((size, 8, 128), lambda i: (i, 0, 0))],
+        out_specs=block,
+        compiler_params=pltpu.CompilerParams(vmem_limit_bytes=VMEM_MIB * 1024 * 1024),
+    )(physics, share)
 
 
 def solution(mesh):

time: 51.7 us -> 56.2 us (1.087)
  Pallas kernels: 48.5 us -> 56 us
  other arithmetic: 2.99 us -> 0 us
    pallas_call x0 -> x1, Pallas kernels: none -> 4.33 us  [subtract(): pl.pallas_call(subtract_kernel, out_shape=jax.ShapeDtypeStruct(physics.sh...]
    pallas_call x1, Pallas kernels: 48.5 us -> 51.6 us  [local(): pl.pallas_call(functools.partial(main_kernel, dims), out_shape=[jax.Shape...]
    sub x1 -> x0, other arithmetic: 2.99 us -> none  [local(): return physics - share.reshape(fields, 1, 8, 128)]
where the time goes in v7:
time: 56.2 us; the launch traced here: 56 us
  Pallas kernels  56 us (100%)
    pallas_call x1, Pallas kernels, local(): pl.pallas_call(functools.partial(main_kernel, dims), out_shape=[jax.Shape...  51.6 us
    pallas_call x1, Pallas kernels, subtract(): pl.pallas_call(subtract_kernel, out_shape=jax.ShapeDtypeStruct(physics.sh...  4.33 us

profile of v7, /device:TPU:0, one launch (start us, length us, event | category | flops | bytes accessed | tf_op | source)
XLA Modules:
  0.0 56.0 jit_solution(2845446376176339052)
XLA Ops:
  0.0 51.6 %shard_map.91 = (f32[15,32,8,128]{3,2,1,0:T(8,128)}, f32[120,128]{1,0:T(8,128)}) custom-call(f32[15,32,8,128]{3,2,1,0:T(8,128)} %state_h.1, s32[8,128]{1,0:T(8,128)} %classes_h.1, s32[1,1024]{1,0:T(1,128)} %bitcast.5, f32[256,256]{1,0:T(8,128)} %constant.4.clone.w_h, f32[7,8,128]{2,1,0:T(8,128)} %constant.5.clone.shifts_h, f32[15]{0:T(128)} %rate_h.1, ...), custom_call_target="tpu_custom_call" | custom-call | tf_op jit(solution)/shard_map/pallas_call | solution.py:727
  51.6 4.3 %shard_map.92 = f32[15,32,8,128]{3,2,1,0:T(8,128)} custom-call(f32[15,32,8,128]{3,2,1,0:T(8,128)} %get-tuple-element.7.physics, f32[15,8,128]{2,1,0:T(8,128)} %bitcast.4), custom_call_target="tpu_custom_call" | custom-call | tf_op jit(solution)/shard_map/pallas_call | solution.py:815

commit v8 on v6

--- a/solution.py
+++ b/solution.py
@@ -12,7 +12,7 @@
 STEPS = 2
 SUBSTEPS = 4
 MESH = pl.DeviceIdType.MESH
-SKEW = 2
+SKEW = 1
 VMEM_MIB = 63
 
 
@@ -204,7 +204,7 @@
     ex, ey, lb = lax.axis_index("ex"), lax.axis_index("ey"), lax.axis_index("lb")
     tile = ex * n_ey + ey
     sides = 1 if n_ey == 2 else 2
-    size = 3 if fields % 3 == 0 else 1
+    size = 5 if fields % 5 == 0 else 1
     chunks = fields // size
 
     def tile_peer(o):
@@ -637,7 +637,7 @@
 
         return c
 
-    lax.fori_loop(chunks, chunks + 2, trailing, 0)
+    lax.fori_loop(chunks, chunks + 1, trailing, 0)
     total = slots[lb]
     for o in range(1, n_lb):
         one_copy(o).wait_recv()
@@ -649,7 +649,7 @@
         return c
 
     lax.fori_loop(1, tiles, start_two, 0)
-    lax.fori_loop(chunks + 2, chunks + 4, trailing, 0)
+    lax.fori_loop(chunks + 1, chunks + 2, trailing, 0)
 
     def add_two(o, c):
         two_copy(o).wait_recv()
@@ -660,7 +660,7 @@
     for o in range(1, n_lb):
         three_copy(o).start()
 
-    lax.fori_loop(chunks + 4, chunks + hops, trailing, 0)
+    lax.fori_loop(chunks + 2, chunks + hops, trailing, 0)
     for o in range(1, n_lb):
         three_arrival(o).wait_recv()
     spread_share = jnp.zeros((48, 1024), jnp.float32)

time: 51.7 us -> 53.2 us (1.029)
  Pallas kernels: 48.5 us -> 50.1 us
    pallas_call x1, Pallas kernels: 48.5 us -> 50.1 us  [local(): pl.pallas_call(functools.partial(main_kernel, dims), out_shape=[jax.Shape...]
where the time goes in v8:
time: 53.2 us; the launch traced here: 53.1 us
  Pallas kernels  50.1 us (94%)
  other arithmetic  2.99 us (6%)
    pallas_call x1, Pallas kernels, local(): pl.pallas_call(functools.partial(main_kernel, dims), out_shape=[jax.Shape...  50.1 us
    sub x1, other arithmetic, local(): return physics - share.reshape(fields, 1, 8, 128)  2.99 us

profile of v8, /device:TPU:0, one launch (start us, length us, event | category | flops | bytes accessed | tf_op | source)
XLA Modules:
  0.0 53.1 jit_solution(3346748060961894672)
XLA Ops:
  0.0 50.1 %shard_map.91 = (f32[15,32,8,128]{3,2,1,0:T(8,128)}, f32[120,128]{1,0:T(8,128)}) custom-call(f32[15,32,8,128]{3,2,1,0:T(8,128)} %state_h.1, s32[8,128]{1,0:T(8,128)} %classes_h.1, s32[1,1024]{1,0:T(1,128)} %bitcast.5, f32[256,256]{1,0:T(8,128)} %constant.4.clone.w_h, f32[7,8,128]{2,1,0:T(8,128)} %constant.5.clone.shifts_h, f32[15]{0:T(128)} %rate_h.1, ...), custom_call_target="tpu_custom_call" | custom-call | tf_op jit(solution)/shard_map/pallas_call | solution.py:727
  50.1 3.0 %broadcast_subtract_fusion = f32[15,32,8,128]{3,2,1,0:T(8,128)} fusion(f32[15,32,8,128]{3,2,1,0:T(8,128)} %get-tuple-element.7, f32[15,8,128]{2,1,0:T(8,128)} %bitcast.4), kind=kLoop, calls=%fused_computation | loop fusion | flops 491520 | bytes 3993600 | tf_op jit(solution)/shard_map/sub | solution.py:804
